TPU v7x, 32 devices: a whole 2x2x4 slice. The times are simulated.
32 devices in a mesh: wide: 4 (over z), narrow: 8 (over y, x, core).
Axes of the slice: x: 2, y: 2, z: 4, core: 2. Of those that a mesh axis runs over, the one named last changes fastest.
Arguments:
- tokens: bfloat16 [4096, 2048], P(('wide', 'narrow')), may hold values from -6 to 6
- out_grad: bfloat16 [4096, 2048], P(('wide', 'narrow')), may hold values from -6 to 6
- expert_ids: int32 [4096, 6], P(('wide', 'narrow')), may hold values from 0 to 15, as said below
- gates: bfloat16 [4096, 6], P(('wide', 'narrow')), may hold values from 0.049804688 to 0.5
- w_gate: bfloat16 [32, 2048, 704], P(('wide', 'narrow')), may hold values from -0.125 to 0.125
- w_up: bfloat16 [32, 2048, 704], P(('wide', 'narrow')), may hold values from -0.125 to 0.125
- w_down: bfloat16 [32, 704, 2048], P(('wide', 'narrow')), may hold values from -0.15625 to 0.15625
- gate_saved: bfloat16 [32, 1536, 704], P(('wide', 'narrow')), may hold values from -6 to 6
- up_saved: bfloat16 [32, 1536, 704], P(('wide', 'narrow')), may hold values from -6 to 6
Outputs:
- token_grad: bfloat16 [4096, 2048], P(('wide', 'narrow'))
- grad_gate: bfloat16 [32, 2048, 704], P(('wide', 'narrow'))
- grad_up: bfloat16 [32, 2048, 704], P(('wide', 'narrow'))
- grad_down: bfloat16 [32, 704, 2048], P(('wide', 'narrow'))
Inputs may be any that keep to these rules, and one draw needn't show every extreme that they name: `expert_ids`: each row names 6 different experts, 2 in each of exactly 3 of the groups of 4 consecutive experts; for every device and every group, exactly 96 of the device's tokens name experts of that group.
All inputs are finite; a program needn't handle non-finite values.
Results may differ from a plain program's by a relative error of at most 0.012.
Values may be sent and summed in bfloat16 or wider, within the bound.
A program may use at most 192 MiB of HBM per device.

v0:
```python
import jax
import jax.numpy as jnp
from jax import lax
from jax.sharding import PartitionSpec as P


def slot_tables(ids, gate_rows, experts, slot_cap):
    count = ids.shape[0]
    flat = ids.reshape(-1)
    picked = (flat[:, None] == jnp.arange(experts, dtype=jnp.int32)[None, :]).astype(jnp.int32)
    before = jnp.cumsum(picked, axis=0) - picked
    rank = jnp.sum(before * picked, axis=1)
    keep = rank < slot_cap
    place = flat * slot_cap + rank
    hits = (jnp.arange(experts * slot_cap, dtype=jnp.int32)[:, None] == place[None, :]) & keep[
        None, :
    ]
    hits = hits.reshape(experts * slot_cap, count, ids.shape[1])
    placed = jnp.any(hits, axis=2).astype(jnp.float32)
    weighted = jnp.sum(jnp.where(hits, gate_rows[None, :, :], jnp.float32(0.0)), axis=2)
    return (placed, weighted)


def send_rows(rows_x, rows_dy):
    got_x, got_dy = (
        lax.all_to_all(rows_x, ("wide", "narrow"), split_axis=0, concat_axis=0, tiled=True),
        lax.all_to_all(rows_dy, ("wide", "narrow"), split_axis=0, concat_axis=0, tiled=True),
    )
    return (got_x, got_dy)


def return_rows(partial_value):
    return lax.all_to_all(
        partial_value.astype(jnp.bfloat16),
        ("wide", "narrow"),
        split_axis=0,
        concat_axis=0,
        tiled=True,
    ).astype(partial_value.dtype)


def local(tokens, out_grad, expert_ids, gates, w_gate, w_up, w_down, gate_saved, up_saved):
    high = lax.Precision.HIGHEST
    n_wide = lax.axis_size("wide")
    n_narrow = lax.axis_size("narrow")
    devices = n_wide * n_narrow
    experts = devices // 2
    width = tokens.shape[1]
    slot_cap = gate_saved.shape[1] // devices
    across = (((0,), (0,)), ((), ()))
    inner = (((1,), (1,)), ((), ()))
    placed, weighted = slot_tables(expert_ids, gates.astype(jnp.float32), experts, slot_cap)
    x_slots = jnp.dot(
        placed.astype(jnp.bfloat16), tokens, preferred_element_type=jnp.float32
    ).astype(jnp.bfloat16)
    dy_slots = jnp.dot(weighted, out_grad.astype(jnp.float32), precision=high).astype(jnp.bfloat16)
    x_slots = x_slots.reshape(experts, slot_cap, width)
    dy_slots = dy_slots.reshape(experts, slot_cap, width)
    mine_x, mine_dy = send_rows(jnp.repeat(x_slots, 2, axis=0), jnp.repeat(dy_slots, 2, axis=0))
    rows_x, rows_dy = (mine_x, mine_dy)
    rows_x = rows_x.reshape(devices * slot_cap, width)
    rows_dy = rows_dy.reshape(devices * slot_cap, width)
    weight_gate = w_gate[0]
    weight_up = w_up[0]
    weight_down = w_down[0]
    gate_pre = gate_saved[0].astype(jnp.float32)
    up_pre = up_saved[0].astype(jnp.float32)
    sigma = jax.nn.sigmoid(gate_pre)
    silu = gate_pre * sigma
    act = (silu * up_pre).astype(jnp.bfloat16)
    act_grad = lax.dot_general(rows_dy, weight_down, inner, preferred_element_type=jnp.float32)
    up_grad = (act_grad * silu).astype(jnp.bfloat16)
    gate_grad = (act_grad * up_pre * sigma * (1.0 + gate_pre * (1.0 - sigma))).astype(jnp.bfloat16)
    partial_value = lax.dot_general(
        gate_grad, weight_gate, inner, preferred_element_type=jnp.float32
    )
    partial_value = partial_value + lax.dot_general(
        up_grad, weight_up, inner, preferred_element_type=jnp.float32
    )
    partial_value = partial_value.reshape(devices, slot_cap, width)
    grad_gate = lax.dot_general(
        rows_x, gate_grad, across, preferred_element_type=jnp.float32
    ).astype(jnp.bfloat16)
    grad_up = lax.dot_general(rows_x, up_grad, across, preferred_element_type=jnp.float32).astype(
        jnp.bfloat16
    )
    grad_down = lax.dot_general(act, rows_dy, across, preferred_element_type=jnp.float32).astype(
        jnp.bfloat16
    )
    arrived = return_rows(partial_value)
    slot_grad = jnp.sum(arrived.reshape(experts, 2, slot_cap, width), axis=1).reshape(
        experts * slot_cap, width
    )
    token_grad = lax.dot_general(
        placed, slot_grad, across, precision=high, preferred_element_type=jnp.float32
    )
    return (token_grad.astype(jnp.bfloat16), grad_gate[None], grad_up[None], grad_down[None])


def solution(mesh):
    return jax.shard_map(
        local,
        mesh=mesh,
        in_specs=(
            P(("wide", "narrow"), None),
            P(("wide", "narrow"), None),
            P(("wide", "narrow"), None),
            P(("wide", "narrow"), None),
            P(("wide", "narrow"), None, None),
            P(("wide", "narrow"), None, None),
            P(("wide", "narrow"), None, None),
            P(("wide", "narrow"), None, None),
            P(("wide", "narrow"), None, None),
        ),
        out_specs=(
            P(("wide", "narrow"), None),
            P(("wide", "narrow"), None, None),
            P(("wide", "narrow"), None, None),
            P(("wide", "narrow"), None, None),
        ),
        check_vma=False,
    )
```

profile of v0, /device:TPU:0, one launch (start us, length us, event | category | flops | bytes accessed | tf_op | source)
XLA Modules:
  0.0 462.3 jit_solution(17696924237024374867)
XLA Ops:
  0.6 0.0 copy-start
  0.6 0.9 copy.29
  1.6 0.1 eq.44
  1.7 0.1 eq.40
  1.9 1.7 reduce-window.6
  3.6 0.3 slice_reduce_fusion
  3.9 0.1 fusion.31
  4.0 0.1 reduce_sum.30
  4.1 0.1 copy.32
  4.2 0.7 multiply_add_fusion
  4.9 0.7 convert_element_type.74
  5.6 0.5 select_reduce_fusion
  6.1 3.8 convolution_convert_fusion.1
  9.9 3.5 broadcast_in_dim.34
  13.4 7.4 %all-to-all-start = ((bf16[32,48,2048]{2,1,0:T(8,128)(2,1)}), bf16[32,48,2048]{2,1,0:T(8,128)(2,1)}, u32[]{:S(2)}, u32[]{:S(2)}) async-start(bf16[32,48,2048]{2,1,0:T(8,128)(2,1)} %bitcast.101), calls=%async_computation | async-start | bytes 12582912 | tf_op jit(solution)/shard_map/all_to_all | solution.py:27
  20.8 0.4 fusion.26
  21.2 2.7 convolution_convert_fusion
  23.9 137.0 %all-to-all-done = bf16[32,48,2048]{2,1,0:T(8,128)(2,1)} async-done(((bf16[32,48,2048]{2,1,0:T(8,128)(2,1)}), bf16[32,48,2048]{2,1,0:T(8,128)(2,1)}, u32[]{:S(2)}, u32[]{:S(2)}) %all-to-all-start) | async-done | bytes 6291488 | tf_op jit(solution)/shard_map/all_to_all | solution.py:27
  160.8 5.5 %broadcast_in_dim.35 = bf16[16,2,48,2048]{3,2,1,0:T(8,128)(2,1)} broadcast(bf16[16,48,2048]{2,1,0:T(8,128)(2,1)} %bitcast.103), dimensions={0,2,3} | broadcast | bytes 9437184 | tf_op jit(solution)/shard_map/broadcast_in_dim | solution.py:59
  166.4 3.8 all-to-all-start.2
  170.2 10.7 %fusion.6 = (bf16[1536,704]{0,1:T(8,128)(2,1)S(1)}, f32[1536,704]{0,1:T(8,128)S(1)}) fusion(bf16[1,1536,704]{1,2,0:T(8,128)(2,1)} %param.17, bf16[1,1536,704]{1,2,0:T(8,128)(2,1)} %param.16, bf16[1536,2048]{1,0:T(8,128)(2,1)} %bitcast.3, bf16[1,704,2048]{2,1,0:T(8,128)(2,1)} %param.15), kind=kOutput, calls=%fused_computation.13 | convolution fusion | flops 4442161152 | bytes 19988480 | tf_op jit(solution)/shard_map/dot_general | solution.py:71
  180.9 0.0 copy-start.7
  181.0 8.1 %fusion.21 = f32[1536,2048]{1,0:T(8,128)} fusion(bf16[1536,704]{0,1:T(8,128)(2,1)S(1)} %get-tuple-element.4, bf16[1,2048,704]{1,2,0:T(8,128)(2,1)S(1)} %copy-done), kind=kOutput, calls=%fused_computation.33 | convolution fusion | flops 4429185024 | bytes 17629184 | tf_op jit(solution)/shard_map/dot_general | solution.py:74
  189.0 10.2 %add_convert_fusion = bf16[1536,2048]{1,0:T(8,128)(2,1)} fusion(f32[1536,2048]{1,0:T(8,128)} %fusion.21, bf16[1,2048,704]{1,2,0:T(8,128)(2,1)S(1)} %copy-done.3, f32[1536,704]{0,1:T(8,128)S(1)} %get-tuple-element.5, bf16[1,1536,704]{1,2,0:T(8,128)(2,1)S(1)} %copy-done.5), kind=kOutput, calls=%fused_computation.1 | convolution fusion | flops 4443045888 | bytes 28246016 | tf_op jit(solution)/shard_map/dot_general | solution.py:77
  199.2 110.8 %all-to-all-done.2 = bf16[32,48,2048]{2,1,0:T(8,128)(2,1)} async-done(((bf16[32,48,2048]{2,1,0:T(8,128)(2,1)}), bf16[32,48,2048]{2,1,0:T(8,128)(2,1)}, u32[]{:S(2)}, u32[]{:S(2)}) %all-to-all-start.2) | async-done | bytes 6291488 | tf_op jit(solution)/shard_map/all_to_all | solution.py:26
  310.0 3.8 all-to-all-start.1
  313.9 9.8 %fusion.18 = bf16[1,2048,704]{1,2,0:T(8,128)(2,1)} fusion(bf16[1536,704]{0,1:T(8,128)(2,1)} %copy-done.7, bf16[1536,2048]{1,0:T(8,128)(2,1)} %bitcast.14), kind=kOutput, calls=%fused_computation.30 | convolution fusion | flops 4430626816 | bytes 11337728 | tf_op jit(solution)/shard_map/dot_general | solution.py:81
  323.7 9.2 %fusion.17 = bf16[1,704,2048]{2,1,0:T(8,128)(2,1)} fusion(bf16[1536,2048]{1,0:T(8,128)(2,1)} %bitcast.3, bf16[1,1536,704]{1,2,0:T(8,128)(2,1)S(1)} %copy-done.4, bf16[1,1536,704]{1,2,0:T(8,128)(2,1)S(1)} %copy-done.6), kind=kOutput, calls=%fused_computation.29 | convolution fusion | flops 4439277568 | bytes 13500416 | tf_op jit(solution)/shard_map/dot_general | solution.py:87
  332.9 9.1 %fusion.19 = bf16[1,2048,704]{1,2,0:T(8,128)(2,1)} fusion(bf16[1536,2048]{1,0:T(8,128)(2,1)} %bitcast.14, f32[1536,704]{0,1:T(8,128)S(1)} %bitcast.108, bf16[1,1536,704]{1,2,0:T(8,128)(2,1)S(1)} %copy-done.6), kind=kOutput, calls=%fused_computation.31 | convolution fusion | flops 4438196224 | bytes 15663104 | tf_op jit(solution)/shard_map/dot_general | solution.py:84
  342.0 111.7 %all-to-all-done.1 = bf16[32,48,2048]{2,1,0:T(8,128)(2,1)} async-done(((bf16[32,48,2048]{2,1,0:T(8,128)(2,1)}), bf16[32,48,2048]{2,1,0:T(8,128)(2,1)}, u32[]{:S(2)}, u32[]{:S(2)}) %all-to-all-start.1) | async-done | bytes 6291488 | tf_op jit(solution)/shard_map/all_to_all | solution.py:33
  453.7 5.3 %convert_reduce_fusion = f32[16,48,2048]{2,1,0:T(8,128)S(1)} fusion(bf16[32,48,2048]{2,1,0:T(8,128)(2,1)} %all-to-all-done.1), kind=kLoop, calls=%fused_computation | loop fusion | flops 4718592 | bytes 12582912 | tf_op jit(solution)/shard_map/reduce_sum | solution.py:91
  459.1 3.2 convolution_convert_fusion.5
  (24 shorter events, 0.1 us)
Async XLA Ops:
  0.6 180.3 %copy-start = (bf16[1,2048,704]{1,2,0:T(8,128)(2,1)S(1)}, bf16[1,2048,704]{1,2,0:T(8,128)(2,1)}, u32[]{:S(2)}) copy-start(bf16[1,2048,704]{1,2,0:T(8,128)(2,1)} %param.13) | copy-start | bytes 8650756
  13.4 7.8 %copy-start.2 = (bf16[128,2048]{1,0:T(8,128)(2,1)S(1)}, bf16[128,2048]{1,0:T(8,128)(2,1)}, u32[]{:S(2)}) copy-start(bf16[128,2048]{1,0:T(8,128)(2,1)} %param.9) | copy-start | bytes 1572868
  13.4 147.4 %all-to-all-start = ((bf16[32,48,2048]{2,1,0:T(8,128)(2,1)}), bf16[32,48,2048]{2,1,0:T(8,128)(2,1)}, u32[]{:S(2)}, u32[]{:S(2)}) async-start(bf16[32,48,2048]{2,1,0:T(8,128)(2,1)} %bitcast.101), calls=%async_computation | async-start | bytes 12582912 | tf_op jit(solution)/shard_map/all_to_all | solution.py:27
  166.4 143.7 %all-to-all-start.2 = ((bf16[32,48,2048]{2,1,0:T(8,128)(2,1)}), bf16[32,48,2048]{2,1,0:T(8,128)(2,1)}, u32[]{:S(2)}, u32[]{:S(2)}) async-start(bf16[32,48,2048]{2,1,0:T(8,128)(2,1)} %bitcast.100), calls=%async_computation.2 | async-start | bytes 12582912 | tf_op jit(solution)/shard_map/all_to_all | solution.py:26
  180.9 8.1 %copy-start.7 = (bf16[1536,704]{0,1:T(8,128)(2,1)}, bf16[1536,704]{0,1:T(8,128)(2,1)S(1)}, u32[]{:S(2)}) copy-start(bf16[1536,704]{0,1:T(8,128)(2,1)S(1)} %get-tuple-element.4) | copy-start | bytes 6488068
  180.9 8.1 %copy-start.8 = (f32[1536,704]{0,1:T(8,128)}, f32[1536,704]{0,1:T(8,128)S(1)}, u32[]{:S(2)}) copy-start(f32[1536,704]{0,1:T(8,128)S(1)} %get-tuple-element.5) | copy-start | bytes 12976132
  180.9 8.1 %copy-start.3 = (bf16[1,2048,704]{1,2,0:T(8,128)(2,1)S(1)}, bf16[1,2048,704]{1,2,0:T(8,128)(2,1)}, u32[]{:S(2)}) copy-start(bf16[1,2048,704]{1,2,0:T(8,128)(2,1)} %param.14) | copy-start | bytes 8650756
  180.9 8.1 %copy-start.5 = (bf16[1,1536,704]{1,2,0:T(8,128)(2,1)S(1)}, bf16[1,1536,704]{1,2,0:T(8,128)(2,1)}, u32[]{:S(2)}) copy-start(bf16[1,1536,704]{1,2,0:T(8,128)(2,1)} %param.16) | copy-start | bytes 6488068
  310.0 143.7 %all-to-all-start.1 = ((bf16[32,48,2048]{2,1,0:T(8,128)(2,1)}), bf16[32,48,2048]{2,1,0:T(8,128)(2,1)}, u32[]{:S(2)}, u32[]{:S(2)}) async-start(bf16[32,48,2048]{2,1,0:T(8,128)(2,1)} %bitcast.105), calls=%async_computation.1 | async-start | bytes 12582912 | tf_op jit(solution)/shard_map/all_to_all | solution.py:33
  313.9 9.8 %copy-start.4 = (bf16[1,1536,704]{1,2,0:T(8,128)(2,1)S(1)}, bf16[1,1536,704]{1,2,0:T(8,128)(2,1)}, u32[]{:S(2)}) copy-start(bf16[1,1536,704]{1,2,0:T(8,128)(2,1)} %param.17) | copy-start | bytes 6488068
  313.9 9.8 %copy-start.6 = (bf16[1,1536,704]{1,2,0:T(8,128)(2,1)S(1)}, bf16[1,1536,704]{1,2,0:T(8,128)(2,1)}, u32[]{:S(2)}) copy-start(bf16[1,1536,704]{1,2,0:T(8,128)(2,1)} %param.16) | copy-start | bytes 6488068
  313.9 19.0 %slice-start = ((s8[4325376]{0:T(1024)(128)(4,1)}), s8[4194304]{0:T(1024)(128)(4,1)S(1)}, s32[]{:S(2)}) async-start(s8[4325376]{0:T(1024)(128)(4,1)} %bitcast.107), calls=%async_computation.3 | async-start | bytes 8388608
  323.7 9.2 %slice-start.1 = ((s8[4325376]{0:T(1024)(128)(4,1)}), s8[131072]{0:T(1024)(128)(4,1)S(1)}, s32[]{:S(2)}) async-start(s8[4325376]{0:T(1024)(128)(4,1)} %bitcast.107), calls=%async_computation.4 | async-start | bytes 262144
  453.7 8.5 %copy-start.1 = (bf16[1,2048,704]{1,2,0:T(8,128)(2,1)S(1)}, bf16[1,2048,704]{1,2,0:T(8,128)(2,1)}, u32[]{:S(2)}) copy-start(bf16[1,2048,704]{1,2,0:T(8,128)(2,1)} %param.13) | copy-start | bytes 8650756
where the time goes:
time: 463 us; the launch traced here: 462 us
  waiting for transfers between devices  359 us (78%)
  matrix products  66.8 us (14%)
  starting transfers between devices  15 us (3%)
  local copies, waits for them, and re-layouts  10.7 us (2%)
  other arithmetic  9.48 us (2%)
    all_to_all x1, waiting for transfers between devices, send_rows(): lax.all_to_all(rows_dy, ('wide', 'narrow'), split_axis=0, concat_axis=0,...  137 us
    all_to_all x1, waiting for transfers between devices, return_rows(): lax.all_to_all(partial_value.astype(jnp.bfloat16), ('wide', 'narrow'), sp...  112 us
    all_to_all x1, waiting for transfers between devices, send_rows(): lax.all_to_all(rows_x, ('wide', 'narrow'), split_axis=0, concat_axis=0, t...  111 us
    dot_general x1, matrix products, local(): lax.dot_general(rows_dy, weight_down, inner, preferred_element_type=jnp.f...  10.7 us
    dot_general x1, matrix products, local(): lax.dot_general(up_grad, weight_up, inner, preferred_element_type=jnp.flo...  10.2 us
    dot_general x1, matrix products, local(): lax.dot_general(rows_x, gate_grad, across, preferred_element_type=jnp.flo...  9.79 us
  transfers between devices with their start and end apart: 3, of which 3 were waited for; matrix products, arithmetic and copies ran while one was open for 13% of the time, Pallas kernels for 0%

commit v1 on v0

v1 whole, which is shorter than its diff:
```python
import jax
import jax.numpy as jnp
from jax import lax
from jax.sharding import PartitionSpec as P

BF = jnp.bfloat16
F32 = jnp.float32
ACROSS = (((0,), (0,)), ((), ()))
INNER = (((1,), (1,)), ((), ()))


def swap(value, axis, shift):
    if shift == 0:
        return value
    size = lax.axis_size(axis)
    return lax.ppermute(value, axis, [(i, i ^ shift) for i in range(size)])


def route_tables(ids, gates, experts, cap):
    count = ids.shape[0]
    hit = ids[:, :, None] == jnp.arange(experts, dtype=jnp.int32)[None, None, :]
    picked = jnp.any(hit, axis=1)
    gate = jnp.sum(jnp.where(hit, gates.astype(F32)[:, :, None], 0.0), axis=1)
    row = lax.broadcasted_iota(jnp.int32, (count, count), 0)
    col = lax.broadcasted_iota(jnp.int32, (count, count), 1)
    rank = jnp.dot((col < row).astype(BF), picked.astype(BF), preferred_element_type=F32)
    rank = jnp.where(picked & (rank < cap), rank, -1.0)
    return picked, rank, gate


def local(tokens, out_grad, expert_ids, gates, w_gate, w_up, w_down, gate_saved, up_saved):
    n_wide = lax.axis_size("wide")
    n_narrow = lax.axis_size("narrow")
    devices = n_wide * n_narrow
    experts = devices // 2
    spots = n_narrow // 2
    count, width = tokens.shape
    half = w_gate.shape[2]
    cap = gate_saved.shape[1] // devices
    rows = count * (expert_ids.shape[1] // 2) // n_wide
    my_wide = lax.axis_index("wide")
    my_narrow = lax.axis_index("narrow")
    my_spot = my_narrow // 2
    me = my_wide * n_narrow + my_narrow

    picked, rank, gate = route_tables(expert_ids, gates, experts, cap)
    groups = my_wide ^ jnp.arange(n_wide, dtype=jnp.int32)
    member = jnp.any(picked.reshape(count, n_wide, spots), axis=2)
    row = lax.broadcasted_iota(jnp.int32, (count, count), 0)
    col = lax.broadcasted_iota(jnp.int32, (count, count), 1)
    place = jnp.dot((col < row).astype(BF), member.astype(BF), preferred_element_type=F32)
    place = jnp.where(member, place, -1.0)
    place = jnp.take(place, groups, axis=1)
    pack = (place[:, :, None] == jnp.arange(rows, dtype=F32)[None, None, :]).astype(BF)
    pack = pack.reshape(count, n_wide * rows)
    info = jnp.concatenate([rank.reshape(count, n_wide, spots), gate.reshape(count, n_wide, spots)], 2)
    info = jnp.take(info, groups, axis=1).astype(BF)

    order = me ^ jnp.arange(devices, dtype=jnp.int32)
    gate_rows = jnp.take(gate_saved[0].reshape(devices, cap, half), order, axis=0)
    up_rows = jnp.take(up_saved[0].reshape(devices, cap, half), order, axis=0)
    gate_rows = gate_rows.reshape(n_wide, n_narrow * cap, half)
    up_rows = up_rows.reshape(n_wide, n_narrow * cap, half)

    spot_order = my_spot ^ jnp.arange(spots, dtype=jnp.int32)
    weight_gate, weight_up, weight_down = w_gate[0], w_up[0], w_down[0]

    arrived = []
    for step in range(n_wide):
        mine = pack[:, step * rows : (step + 1) * rows]
        sent_x = lax.dot_general(mine, tokens, ACROSS, preferred_element_type=F32).astype(BF)
        sent_dy = lax.dot_general(mine, out_grad, ACROSS, preferred_element_type=F32).astype(BF)
        sent_info = lax.dot_general(mine, info[:, step], ACROSS, preferred_element_type=F32).astype(BF)
        sent_info = jnp.pad(sent_info, ((0, 0), (0, 128 - 2 * spots)))
        sent = jnp.concatenate([sent_x, sent_dy, sent_info], axis=1)
        arrived.append(swap(sent, "wide", step))

    tables, all_x, all_dy, all_act, all_gate, all_up, partials = [], [], [], [], [], [], []
    for step in range(n_wide):
        got = arrived[step]
        got_rank = jnp.take(got[:, 2 * width : 2 * width + spots], spot_order, axis=1).astype(F32)
        got_gate = jnp.take(got[:, 2 * width + spots : 2 * width + 2 * spots], spot_order, axis=1)
        hits = got_rank[:, :, None] == jnp.arange(cap, dtype=F32)[None, None, :]
        table = hits.astype(BF).reshape(rows, spots * cap)
        scaled = jnp.where(hits, got_gate[:, :, None], jnp.zeros((), BF)).reshape(rows, spots * cap)
        tables.append(table)
        x_slot = lax.dot_general(table, got[:, :width], ACROSS, preferred_element_type=F32).astype(BF)
        dy_slot = lax.dot_general(
            scaled, got[:, width : 2 * width], ACROSS, preferred_element_type=F32
        ).astype(BF)
        both = jnp.stack([x_slot.reshape(spots, cap, width), dy_slot.reshape(spots, cap, width)], 1)
        plane = jnp.stack([swap(both[k], "narrow", 2 * k) for k in range(spots)])
        chip = jnp.stack([plane, swap(plane, "narrow", 1)], 1)
        rows_x = chip[:, :, 0].reshape(n_narrow * cap, width)
        rows_dy = chip[:, :, 1].reshape(n_narrow * cap, width)
        gate_pre = gate_rows[step].astype(F32)
        up_pre = up_rows[step].astype(F32)
        sigma = jax.nn.sigmoid(gate_pre)
        silu = gate_pre * sigma
        act = (silu * up_pre).astype(BF)
        act_grad = lax.dot_general(rows_dy, weight_down, INNER, preferred_element_type=F32)
        up_grad = (act_grad * silu).astype(BF)
        gate_grad = (act_grad * up_pre * sigma * (1.0 + gate_pre * (1.0 - sigma))).astype(BF)
        partial = lax.dot_general(gate_grad, weight_gate, INNER, preferred_element_type=F32)
        partial = partial + lax.dot_general(up_grad, weight_up, INNER, preferred_element_type=F32)
        all_x.append(rows_x)
        all_dy.append(rows_dy)
        all_act.append(act)
        all_gate.append(gate_grad)
        all_up.append(up_grad)
        partials.append(partial.astype(BF).reshape(spots, 2, cap, width))

    token_grad = jnp.zeros((count, width), F32)
    for step in range(n_wide):
        partial = partials[step]
        whole = partial[:, 0].astype(F32) + swap(partial[:, 1], "narrow", 1).astype(F32)
        whole = whole.astype(BF)
        back = jnp.concatenate([swap(whole[k], "narrow", 2 * k) for k in range(spots)], 0)
        part = jnp.dot(tables[step], back, preferred_element_type=F32).astype(BF)
        part = swap(part, "wide", step)
        token_grad = token_grad + jnp.dot(
            pack[:, step * rows : (step + 1) * rows], part, preferred_element_type=F32
        )

    cat_x = jnp.concatenate(all_x, 0)
    cat_dy = jnp.concatenate(all_dy, 0)
    cat_act = jnp.concatenate(all_act, 0)
    cat_gate = jnp.concatenate(all_gate, 0)
    cat_up = jnp.concatenate(all_up, 0)
    grad_gate = lax.dot_general(cat_x, cat_gate, ACROSS, preferred_element_type=F32).astype(BF)
    grad_up = lax.dot_general(cat_x, cat_up, ACROSS, preferred_element_type=F32).astype(BF)
    grad_down = lax.dot_general(cat_act, cat_dy, ACROSS, preferred_element_type=F32).astype(BF)
    return (token_grad.astype(BF), grad_gate[None], grad_up[None], grad_down[None])


def solution(mesh):
    row = P(("wide", "narrow"), None)
    slab = P(("wide", "narrow"), None, None)
    return jax.shard_map(
        local,
        mesh=mesh,
        in_specs=(row, row, row, row, slab, slab, slab, slab, slab),
        out_specs=(row, slab, slab, slab),
        check_vma=False,
    )
```

time: 463 us -> 301 us (0.65)
  waiting for transfers between devices: 359 us -> 80.7 us
  local copies, waits for them, and re-layouts: 10.7 us -> 56.7 us
  other arithmetic: 9.48 us -> 42.5 us
  starting transfers between devices: 15 us -> 40.1 us
  matrix products: 66.8 us -> 74.9 us
    all_to_all x3 -> x0, waiting for transfers between devices: 359 us -> none  [the longest x1 137 us: send_rows(): lax.all_to_all(rows_dy, ('wide', 'narrow'), split_axis=0, concat_axis=0,...]
    ppermute x0 -> x38, waiting for transfers between devices: none -> 80.7 us  [swap(): return lax.ppermute(value, axis, [(i, i ^ shift) for i in range(size)])]
    ppermute x0 -> x38, starting transfers between devices: none -> 40.1 us  [swap(): return lax.ppermute(value, axis, [(i, i ^ shift) for i in range(size)])]
    convert_element_type x0 -> x8, local copies, waits for them, and re-layouts: none -> 21 us  [the longest x4 10.6 us: local(): gate_pre = gate_rows[step].astype(F32)]
    convert_element_type x2 -> x14, other arithmetic: 0.69 us -> 20.4 us  [the longest x4 8.61 us: local(): gate_pre = gate_rows[step].astype(F32)]
    all_to_all x3 -> x0, starting transfers between devices: 15 us -> none  [the longest x1 7.41 us: send_rows(): lax.all_to_all(rows_dy, ('wide', 'narrow'), split_axis=0, concat_axis=0,...]
    unnamed x23 -> x79, local copies, waits for them, and re-layouts: 1.01 us -> 14.8 us
    gather x0 -> x12, local copies, waits for them, and re-layouts: none -> 13.3 us  [the longest x1 3.77 us: local(): up_rows = jnp.take(up_saved[0].reshape(devices, cap, half), order, axis=0)]
  transfers between devices with their start and end apart: 3 -> 38, of which waited for: 3 -> 19; matrix products, arithmetic and copies ran while one was open for 13% -> 51% of each run, Pallas kernels for 0% -> 0%
where the time goes in v1:
time: 301 us; the launch traced here: 296 us
  waiting for transfers between devices  80.7 us (27%)
  matrix products  74.9 us (25%)
  local copies, waits for them, and re-layouts  56.7 us (19%)
  other arithmetic  42.5 us (14%)
  starting transfers between devices  40.1 us (13%)
    ppermute x38, waiting for transfers between devices, swap(): return lax.ppermute(value, axis, [(i, i ^ shift) for i in range(size)])  80.7 us
    ppermute x38, starting transfers between devices, swap(): return lax.ppermute(value, axis, [(i, i ^ shift) for i in range(size)])  40.1 us
    unnamed x79, local copies, waits for them, and re-layouts  14.8 us
    dot_general x4, matrix products, local(): lax.dot_general(rows_dy, weight_down, INNER, preferred_element_type=F32)  12.4 us
    convert_element_type x4, local copies, waits for them, and re-layouts, local(): gate_pre = gate_rows[step].astype(F32)  10.6 us
    convert_element_type x4, local copies, waits for them, and re-layouts, local(): up_pre = up_rows[step].astype(F32)  10.4 us
    convert_element_type x4, other arithmetic, local(): gate_pre = gate_rows[step].astype(F32)  8.61 us
    dot_general x1, matrix products, local(): lax.dot_general(cat_x, cat_gate, ACROSS, preferred_element_type=F32)  8.49 us
  transfers between devices with their start and end apart: 38, of which 19 were waited for; matrix products, arithmetic and copies ran while one was open for 51% of the time, Pallas kernels for 0%

profile of v1, /device:TPU:0, one launch (start us, length us, event | category | flops | bytes accessed | tf_op | source)
XLA Modules:
  0.0 296.4 jit_solution(17667688123602685184)
XLA Ops:
  7.7 3.0 %collective-permute-start.8 = (bf16[96,4224]{1,0:T(8,128)(2,1)}, bf16[96,4224]{1,0:T(8,128)(2,1)}, u32[]{:S(2)}, u32[]{:S(2)}) collective-permute-start(bf16[96,4224]{1,0:T(8,128)(2,1)} %fusion.87), channel_id=1, source_target_pairs={{0,8},{8,0},{16,24},{24,16},{1,9},{9,1},{17,25},{25,17},{2,10},{10... | collective-permute-start | bytes 2433032 | tf_op jit(solution)/shard_map/ppermute | solution.py:16
  23.5 4.2 %copy.175 = bf16[1,1536,704]{2,1,0:T(8,128)(2,1)} copy(bf16[1,1536,704]{1,2,0:T(8,128)(2,1)} %param.21) | data formatting | bytes 4325376 | tf_op args[8]
  27.7 4.3 %copy.177 = bf16[1,1536,704]{2,1,0:T(8,128)(2,1)} copy(bf16[1,1536,704]{1,2,0:T(8,128)(2,1)} %param.20) | data formatting | bytes 4325376 | tf_op args[7]
  32.0 3.8 %gather_fusion.4 = bf16[32,48,704]{2,1,0:T(8,128)(2,1)} fusion(bf16[32,48,704]{2,1,0:T(8,128)(2,1)} %bitcast.360, s32[1024]{0:T(1024)S(1)} %pad_clamp_fusion), kind=kCustom, calls=%fused_computation.1.clone | custom fusion | bytes 4325504 | tf_op jit(solution)/shard_map/jit(_take)/gather | solution.py:61
  35.8 3.8 %gather_fusion.5 = bf16[32,48,704]{2,1,0:T(8,128)(2,1)} fusion(bf16[32,48,704]{2,1,0:T(8,128)(2,1)} %bitcast.359, s32[1024]{0:T(1024)S(1)} %pad_clamp_fusion), kind=kCustom, calls=%fused_computation.9.clone | custom fusion | bytes 4325504 | tf_op jit(solution)/shard_map/jit(_take)/gather | solution.py:60
  39.6 2.9 broadcast_select_fusion.1
  45.6 2.6 copy.205
  50.4 2.7 copy.206
  55.2 2.6 copy.191
  64.7 2.6 copy.176
  69.5 2.6 copy.178
  74.3 2.6 copy.219
  79.1 2.6 copy.220
  111.1 6.4 %collective-permute-done.20 = bf16[2,48,2048]{2,1,0:T(8,128)(2,1)} collective-permute-done((bf16[2,48,2048]{2,1,0:T(8,128)(2,1)}, bf16[2,48,2048]{2,1,0:T(8,128)(2,1)}, u32[]{:S(2)}, u32[]{:S(2)}) %collective-permute-start.20) | collective-permute-done | bytes 393248 | tf_op jit(solution)/shard_map/ppermute | solution.py:16
  122.2 2.7 collective-permute-done.9
  127.7 4.9 %collective-permute-done.10 = bf16[2,48,2048]{2,1,0:T(8,128)(2,1)} collective-permute-done((bf16[2,48,2048]{2,1,0:T(8,128)(2,1)}, bf16[2,48,2048]{2,1,0:T(8,128)(2,1)}, u32[]{:S(2)}, u32[]{:S(2)}) %collective-permute-start.10) | collective-permute-done | bytes 393248 | tf_op jit(solution)/shard_map/ppermute | solution.py:16
  134.2 2.8 collective-permute-start.29
  137.0 4.7 %collective-permute-done = bf16[2,48,2048]{2,1,0:T(8,128)(2,1)S(1)} collective-permute-done((bf16[2,48,2048]{2,1,0:T(8,128)(2,1)S(1)}, bf16[2,48,2048]{2,1,0:T(8,128)(2,1)S(1)}, u32[]{:S(2)}, u32[]{:S(2)}) %collective-permute-start) | collective-permute-done | bytes 393248 | tf_op jit(solution)/shard_map/ppermute | solution.py:16
  143.2 6.2 %collective-permute-done.1 = bf16[2,48,2048]{2,1,0:T(8,128)(2,1)S(1)} collective-permute-done((bf16[2,48,2048]{2,1,0:T(8,128)(2,1)S(1)}, bf16[2,48,2048]{2,1,0:T(8,128)(2,1)S(1)}, u32[]{:S(2)}, u32[]{:S(2)}) %collective-permute-start.1) | collective-permute-done | bytes 393248 | tf_op jit(solution)/shard_map/ppermute | solution.py:16
  151.3 7.2 %collective-permute-done.29 = bf16[2,48,2048]{2,1,0:T(8,128)(2,1)S(1)} collective-permute-done((bf16[2,48,2048]{2,1,0:T(8,128)(2,1)S(1)}, bf16[2,48,2048]{2,1,0:T(8,128)(2,1)S(1)}, u32[]{:S(2)}, u32[]{:S(2)}) %collective-permute-start.29) | collective-permute-done | bytes 393248 | tf_op jit(solution)/shard_map/ppermute | solution.py:16
  158.6 7.4 %collective-permute-done.30 = bf16[2,48,2048]{2,1,0:T(8,128)(2,1)S(1)} collective-permute-done((bf16[2,48,2048]{2,1,0:T(8,128)(2,1)S(1)}, bf16[2,48,2048]{2,1,0:T(8,128)(2,1)S(1)}, u32[]{:S(2)}, u32[]{:S(2)}) %collective-permute-start.30) | collective-permute-done | bytes 393248 | tf_op jit(solution)/shard_map/ppermute | solution.py:16
  167.9 3.1 %multiply_convert_fusion.1 = (bf16[384,704]{0,1:T(8,128)(2,1)}, bf16[384,704]{0,1:T(8,128)(2,1)S(1)}, bf16[384,704]{0,1:T(8,128)(2,1)S(1)}) fusion(f32[384,704]{0,1:T(8,128)S(1)} %copy-done.20, f32[384,704]{0,1:T(8,128)S(1)} %copy-done.21, bf16[384,2048]{1,0:T(8,128)(2,1)S(1)} %bitcast.378, bf16[1,704,2048]{2,1,0:T(8,128)(2,1)S(1)} %copy-done), kind=kOutput, calls=%fused_computation.165 | convolution fusion | flops 1111351296 | bytes 8241152 | tf_op jit(solution)/shard_map/dot_general | solution.py:101
  178.2 2.8 multiply_convert_fusion.2
  187.1 3.0 %multiply_convert_fusion.3 = (bf16[384,704]{0,1:T(8,128)(2,1)}, bf16[384,704]{0,1:T(8,128)(2,1)}, bf16[384,704]{0,1:T(8,128)(2,1)S(1)}) fusion(f32[384,704]{0,1:T(8,128)S(1)} %copy-done.16, f32[384,704]{0,1:T(8,128)S(1)} %copy-done.17, bf16[384,2048]{1,0:T(8,128)(2,1)S(1)} %bitcast.387, bf16[1,704,2048]{2,1,0:T(8,128)(2,1)S(1)} %copy-done), kind=kOutput, calls=%fused_computation.167 | convolution fusion | flops 1111351296 | bytes 8241152 | tf_op jit(solution)/shard_map/dot_general | solution.py:101
  193.8 3.4 %multiply_convert_fusion = (bf16[384,704]{0,1:T(8,128)(2,1)}, bf16[384,704]{0,1:T(8,128)(2,1)}, bf16[384,704]{0,1:T(8,128)(2,1)S(1)}) fusion(f32[384,704]{0,1:T(8,128)S(1)} %copy-done.14, f32[384,704]{0,1:T(8,128)S(1)} %copy-done.15, bf16[384,2048]{1,0:T(8,128)(2,1)S(1)} %bitcast.391, bf16[1,704,2048]{2,1,0:T(8,128)(2,1)S(1)} %copy-done), kind=kOutput, calls=%fused_computation.164 | convolution fusion | flops 1111351296 | bytes 8241152 | tf_op jit(solution)/shard_map/dot_general | solution.py:101
  198.6 8.3 %fusion.12 = bf16[1,2048,704]{1,2,0:T(8,128)(2,1)} fusion(bf16[384,704]{0,1:T(8,128)(2,1)S(1)} %get-tuple-element.33, bf16[384,704]{0,1:T(8,128)(2,1)S(1)} %get-tuple-element.30, bf16[384,704]{0,1:T(8,128)(2,1)S(1)} %get-tuple-element.27, bf16[384,704]{0,1:T(8,128)(2,1)S(1)} %get-tuple-element.24, bf16[384,2048]{1,0:T(8,128)(2,1)} %bitcast.395, ...), kind=kOutput, calls=%fused_computation.37 | convolution fusion | flops 4464443392 | bytes 11337728 | tf_op jit(solution)/shard_map/dot_general | solution.py:131
  206.9 8.5 %fusion.11 = bf16[1,2048,704]{1,2,0:T(8,128)(2,1)} fusion(bf16[384,704]{0,1:T(8,128)(2,1)} %get-tuple-element.32, bf16[384,704]{0,1:T(8,128)(2,1)S(1)} %copy-done.24, bf16[384,704]{0,1:T(8,128)(2,1)S(1)} %copy-done.26, bf16[384,704]{0,1:T(8,128)(2,1)} %get-tuple-element.23, bf16[384,2048]{1,0:T(8,128)(2,1)} %bitcast.396, ...), kind=kOutput, calls=%fused_computation.36 | convolution fusion | flops 4464443392 | bytes 11337728 | tf_op jit(solution)/shard_map/dot_general | solution.py:130
  220.9 7.7 %fusion.13 = bf16[1,704,2048]{2,1,0:T(8,128)(2,1)} fusion(bf16[384,2048]{1,0:T(8,128)(2,1)S(1)} %bitcast.392, bf16[384,2048]{1,0:T(8,128)(2,1)S(1)} %bitcast.379, bf16[384,2048]{1,0:T(8,128)(2,1)S(1)} %bitcast.381, bf16[384,2048]{1,0:T(8,128)(2,1)S(1)} %bitcast.388, bf16[384,704]{0,1:T(8,128)(2,1)} %get-tuple-element.31, ...), kind=kOutput, calls=%fused_computation.38 | convolution fusion | flops 4464443392 | bytes 11337728 | tf_op jit(solution)/shard_map/dot_general | solution.py:132
  239.5 6.7 %collective-permute-done.34 = bf16[48,2048]{1,0:T(8,128)(2,1)S(1)} collective-permute-done((bf16[48,2048]{1,0:T(8,128)(2,1)S(1)}, bf16[48,2048]{1,0:T(8,128)(2,1)S(1)}, u32[]{:S(2)}, u32[]{:S(2)}) %collective-permute-start.34) | collective-permute-done | bytes 196640 | tf_op jit(solution)/shard_map/ppermute | solution.py:16
  249.2 6.2 %collective-permute-done.36 = bf16[48,2048]{1,0:T(8,128)(2,1)S(1)} collective-permute-done((bf16[48,2048]{1,0:T(8,128)(2,1)S(1)}, bf16[48,2048]{1,0:T(8,128)(2,1)S(1)}, u32[]{:S(2)}, u32[]{:S(2)}) %collective-permute-start.36) | collective-permute-done | bytes 196640 | tf_op jit(solution)/shard_map/ppermute | solution.py:16
  274.9 11.2 %collective-permute-done.17 = bf16[96,2048]{1,0:T(8,128)(2,1)S(1)} collective-permute-done((bf16[96,2048]{1,0:T(8,128)(2,1)S(1)}, bf16[96,2048]{1,0:T(8,128)(2,1)S(1)}, u32[]{:S(2)}, u32[]{:S(2)}) %collective-permute-start.17) | collective-permute-done | bytes 393248 | tf_op jit(solution)/shard_map/ppermute | solution.py:16
  286.4 7.7 %collective-permute-done.27 = bf16[96,2048]{1,0:T(8,128)(2,1)} collective-permute-done((bf16[96,2048]{1,0:T(8,128)(2,1)}, bf16[96,2048]{1,0:T(8,128)(2,1)}, u32[]{:S(2)}, u32[]{:S(2)}) %collective-permute-start.27) | collective-permute-done | bytes 393248 | tf_op jit(solution)/shard_map/ppermute | solution.py:16
  (256 shorter events, 143.6 us)
Async XLA Ops:
  7.7 74.0 %collective-permute-start.8 = (bf16[96,4224]{1,0:T(8,128)(2,1)}, bf16[96,4224]{1,0:T(8,128)(2,1)}, u32[]{:S(2)}, u32[]{:S(2)}) collective-permute-start(bf16[96,4224]{1,0:T(8,128)(2,1)} %fusion.87), channel_id=1, source_target_pairs={{0,8},{8,0},{16,24},{24,16},{1,9},{9,1},{17,25},{25,17},{2,10},{10... | collective-permute-start | bytes 2433032 | tf_op jit(solution)/shard_map/ppermute | solution.py:16
  15.1 68.8 %collective-permute-start.28 = (bf16[96,4224]{1,0:T(8,128)(2,1)}, bf16[96,4224]{1,0:T(8,128)(2,1)}, u32[]{:S(2)}, u32[]{:S(2)}) collective-permute-start(bf16[96,4224]{1,0:T(8,128)(2,1)} %fusion.89), channel_id=1, source_target_pairs={{0,24},{8,16},{16,8},{24,0},{1,25},{9,17},{17,9},{25,1},{2,26},{10... | collective-permute-start | bytes 2433032 | tf_op jit(solution)/shard_map/ppermute | solution.py:16
  22.0 66.0 %collective-permute-start.18 = (bf16[96,4224]{1,0:T(8,128)(2,1)}, bf16[96,4224]{1,0:T(8,128)(2,1)}, u32[]{:S(2)}, u32[]{:S(2)}) collective-permute-start(bf16[96,4224]{1,0:T(8,128)(2,1)} %fusion.88), channel_id=1, source_target_pairs={{0,16},{8,24},{16,0},{24,8},{1,17},{9,25},{17,1},{25,9},{2,18},{10... | collective-permute-start | bytes 2433032 | tf_op jit(solution)/shard_map/ppermute | solution.py:16
  95.6 15.1 %collective-permute-start.19 = (bf16[2,48,2048]{2,1,0:T(8,128)(2,1)}, bf16[2,48,2048]{2,1,0:T(8,128)(2,1)}, u32[]{:S(2)}, u32[]{:S(2)}) collective-permute-start(bf16[2,48,2048]{2,1,0:T(8,128)(2,1)} %get-tuple-element.37), channel_id=1, source_target_pairs={{0,2},{1,3},{2,0},{3,1},{4,6},{5,7},{6,4},{7,5},{8,10},{9,11},{10,... | collective-permute-start | bytes 1179656 | tf_op jit(solution)/shard_map/ppermute | solution.py:16
  97.1 20.5 %collective-permute-start.20 = (bf16[2,48,2048]{2,1,0:T(8,128)(2,1)}, bf16[2,48,2048]{2,1,0:T(8,128)(2,1)}, u32[]{:S(2)}, u32[]{:S(2)}) collective-permute-start(bf16[2,48,2048]{2,1,0:T(8,128)(2,1)} %get-tuple-element.39), channel_id=1, source_target_pairs={{0,4},{1,5},{2,6},{3,7},{4,0},{5,1},{6,2},{7,3},{8,12},{9,13},{10,... | collective-permute-start | bytes 1179656 | tf_op jit(solution)/shard_map/ppermute | solution.py:16
  98.6 19.0 %collective-permute-start.21 = (bf16[2,48,2048]{2,1,0:T(8,128)(2,1)}, bf16[2,48,2048]{2,1,0:T(8,128)(2,1)}, u32[]{:S(2)}, u32[]{:S(2)}) collective-permute-start(bf16[2,48,2048]{2,1,0:T(8,128)(2,1)} %get-tuple-element.38), channel_id=1, source_target_pairs={{0,6},{1,7},{2,4},{3,5},{4,2},{5,3},{6,0},{7,1},{8,14},{9,15},{10,... | collective-permute-start | bytes 1179656 | tf_op jit(solution)/shard_map/ppermute | solution.py:16
  103.0 21.9 %collective-permute-start.9 = (bf16[2,48,2048]{2,1,0:T(8,128)(2,1)}, bf16[2,48,2048]{2,1,0:T(8,128)(2,1)}, u32[]{:S(2)}, u32[]{:S(2)}) collective-permute-start(bf16[2,48,2048]{2,1,0:T(8,128)(2,1)} %get-tuple-element.43), channel_id=1, source_target_pairs={{0,2},{1,3},{2,0},{3,1},{4,6},{5,7},{6,4},{7,5},{8,10},{9,11},{10,... | collective-permute-start | bytes 1179656 | tf_op jit(solution)/shard_map/ppermute | solution.py:16
  104.5 28.2 %collective-permute-start.10 = (bf16[2,48,2048]{2,1,0:T(8,128)(2,1)}, bf16[2,48,2048]{2,1,0:T(8,128)(2,1)}, u32[]{:S(2)}, u32[]{:S(2)}) collective-permute-start(bf16[2,48,2048]{2,1,0:T(8,128)(2,1)} %get-tuple-element.45), channel_id=1, source_target_pairs={{0,4},{1,5},{2,6},{3,7},{4,0},{5,1},{6,2},{7,3},{8,12},{9,13},{10,... | collective-permute-start | bytes 1179656 | tf_op jit(solution)/shard_map/ppermute | solution.py:16
  110.7 23.5 %collective-permute-start.11 = (bf16[2,48,2048]{2,1,0:T(8,128)(2,1)}, bf16[2,48,2048]{2,1,0:T(8,128)(2,1)S(1)}, u32[]{:S(2)}, u32[]{:S(2)}) collective-permute-start(bf16[2,48,2048]{2,1,0:T(8,128)(2,1)} %get-tuple-element.44), channel_id=1, source_target_pairs={{0,6},{1,7},{2,4},{3,5},{4,2},{5,3},{6,0},{7,1},{8,14},{9,15},{10,... | collective-permute-start | bytes 1179656 | tf_op jit(solution)/shard_map/ppermute | solution.py:16
  119.2 47.1 %collective-permute-start.22 = (bf16[4,2,48,2048]{3,2,0,1:T(8,128)(2,1)S(1)}, bf16[4,2,48,2048]{3,2,0,1:T(8,128)(2,1)S(1)}, u32[]{:S(2)}, u32[]{:S(2)}) collective-permute-start(bf16[4,2,48,2048]{3,2,0,1:T(8,128)(2,1)S(1)} %get-tuple-element.34), channel_id=1, source_target_pairs={{0,1},{1,0},{2,3},{3,2},{4,5},{5,4},{6,7},{7,6},{8,9},{9,8},{10,11... | collective-permute-start | bytes 4718600 | tf_op jit(solution)/shard_map/ppermute | solution.py:16
  119.5 22.2 %collective-permute-start = (bf16[2,48,2048]{2,1,0:T(8,128)(2,1)S(1)}, bf16[2,48,2048]{2,1,0:T(8,128)(2,1)S(1)}, u32[]{:S(2)}, u32[]{:S(2)}) collective-permute-start(bf16[2,48,2048]{2,1,0:T(8,128)(2,1)S(1)} %get-tuple-element.49), channel_id=1, source_target_pairs={{0,2},{1,3},{2,0},{3,1},{4,6},{5,7},{6,4},{7,5},{8,10},{9,11},{10,... | collective-permute-start | bytes 1179656 | tf_op jit(solution)/shard_map/ppermute | solution.py:16
  124.9 24.5 %collective-permute-start.1 = (bf16[2,48,2048]{2,1,0:T(8,128)(2,1)S(1)}, bf16[2,48,2048]{2,1,0:T(8,128)(2,1)S(1)}, u32[]{:S(2)}, u32[]{:S(2)}) collective-permute-start(bf16[2,48,2048]{2,1,0:T(8,128)(2,1)S(1)} %get-tuple-element.51), channel_id=1, source_target_pairs={{0,4},{1,5},{2,6},{3,7},{4,0},{5,1},{6,2},{7,3},{8,12},{9,13},{10,... | collective-permute-start | bytes 1179656 | tf_op jit(solution)/shard_map/ppermute | solution.py:16
  132.7 18.4 %collective-permute-start.2 = (bf16[2,48,2048]{2,1,0:T(8,128)(2,1)S(1)}, bf16[2,48,2048]{2,1,0:T(8,128)(2,1)S(1)}, u32[]{:S(2)}, u32[]{:S(2)}) collective-permute-start(bf16[2,48,2048]{2,1,0:T(8,128)(2,1)S(1)} %get-tuple-element.50), channel_id=1, source_target_pairs={{0,6},{1,7},{2,4},{3,5},{4,2},{5,3},{6,0},{7,1},{8,14},{9,15},{10,... | collective-permute-start | bytes 1179656 | tf_op jit(solution)/shard_map/ppermute | solution.py:16
  134.2 24.4 %collective-permute-start.29 = (bf16[2,48,2048]{2,1,0:T(8,128)(2,1)S(1)}, bf16[2,48,2048]{2,1,0:T(8,128)(2,1)S(1)}, u32[]{:S(2)}, u32[]{:S(2)}) collective-permute-start(bf16[2,48,2048]{2,1,0:T(8,128)(2,1)S(1)} %get-tuple-element.55), channel_id=1, source_target_pairs={{0,2},{1,3},{2,0},{3,1},{4,6},{5,7},{6,4},{7,5},{8,10},{9,11},{10,... | collective-permute-start | bytes 1179656 | tf_op jit(solution)/shard_map/ppermute | solution.py:16
  141.7 24.3 %collective-permute-start.30 = (bf16[2,48,2048]{2,1,0:T(8,128)(2,1)S(1)}, bf16[2,48,2048]{2,1,0:T(8,128)(2,1)S(1)}, u32[]{:S(2)}, u32[]{:S(2)}) collective-permute-start(bf16[2,48,2048]{2,1,0:T(8,128)(2,1)S(1)} %get-tuple-element.57), channel_id=1, source_target_pairs={{0,4},{1,5},{2,6},{3,7},{4,0},{5,1},{6,2},{7,3},{8,12},{9,13},{10,... | collective-permute-start | bytes 1179656 | tf_op jit(solution)/shard_map/ppermute | solution.py:16
  149.4 16.6 %collective-permute-start.31 = (bf16[2,48,2048]{2,1,0:T(8,128)(2,1)S(1)}, bf16[2,48,2048]{2,1,0:T(8,128)(2,1)S(1)}, u32[]{:S(2)}, u32[]{:S(2)}) collective-permute-start(bf16[2,48,2048]{2,1,0:T(8,128)(2,1)S(1)} %get-tuple-element.56), channel_id=1, source_target_pairs={{0,6},{1,7},{2,4},{3,5},{4,2},{5,3},{6,0},{7,1},{8,14},{9,15},{10,... | collective-permute-start | bytes 1179656 | tf_op jit(solution)/shard_map/ppermute | solution.py:16
  151.1 24.9 %collective-permute-start.12 = (bf16[4,2,48,2048]{3,2,0,1:T(8,128)(2,1)S(1)}, bf16[4,2,48,2048]{3,2,0,1:T(8,128)(2,1)S(1)}, u32[]{:S(2)}, u32[]{:S(2)}) collective-permute-start(bf16[4,2,48,2048]{3,2,0,1:T(8,128)(2,1)S(1)} %get-tuple-element.40), channel_id=1, source_target_pairs={{0,1},{1,0},{2,3},{3,2},{4,5},{5,4},{6,7},{7,6},{8,9},{9,8},{10,11... | collective-permute-start | bytes 4718600 | tf_op jit(solution)/shard_map/ppermute | solution.py:16
  158.6 26.4 %collective-permute-start.3 = (bf16[4,2,48,2048]{3,2,0,1:T(8,128)(2,1)S(1)}, bf16[4,2,48,2048]{3,2,0,1:T(8,128)(2,1)S(1)}, u32[]{:S(2)}, u32[]{:S(2)}) collective-permute-start(bf16[4,2,48,2048]{3,2,0,1:T(8,128)(2,1)S(1)} %get-tuple-element.46), channel_id=1, source_target_pairs={{0,1},{1,0},{2,3},{3,2},{4,5},{5,4},{6,7},{7,6},{8,9},{9,8},{10,11... | collective-permute-start | bytes 4718600 | tf_op jit(solution)/shard_map/ppermute | solution.py:16
  166.3 25.4 %collective-permute-start.32 = (bf16[4,2,48,2048]{3,2,0,1:T(8,128)(2,1)S(1)}, bf16[4,2,48,2048]{3,2,0,1:T(8,128)(2,1)S(1)}, u32[]{:S(2)}, u32[]{:S(2)}) collective-permute-start(bf16[4,2,48,2048]{3,2,0,1:T(8,128)(2,1)S(1)} %get-tuple-element.52), channel_id=1, source_target_pairs={{0,1},{1,0},{2,3},{3,2},{4,5},{5,4},{6,7},{7,6},{8,9},{9,8},{10,11... | collective-permute-start | bytes 4718600 | tf_op jit(solution)/shard_map/ppermute | solution.py:16
  175.5 53.0 %collective-permute-start.23 = (bf16[4,48,2048]{2,1,0:T(8,128)(2,1)}, bf16[4,48,2048]{2,1,0:T(8,128)(2,1)}, u32[]{:S(2)}, u32[]{:S(2)}) collective-permute-start(bf16[4,48,2048]{2,1,0:T(8,128)(2,1)} %slice_bitcast_fusion.2), channel_id=1, source_target_pairs={{0,1},{1,0},{2,3},{3,2},{4,5},{5,4},{6,7},{7,6},{8,9},{9,8},{10,11... | collective-permute-start | bytes 2359304 | tf_op jit(solution)/shard_map/ppermute | solution.py:16
  185.0 49.1 %collective-permute-start.13 = (bf16[4,48,2048]{2,1,0:T(8,128)(2,1)}, bf16[4,48,2048]{2,1,0:T(8,128)(2,1)}, u32[]{:S(2)}, u32[]{:S(2)}) collective-permute-start(bf16[4,48,2048]{2,1,0:T(8,128)(2,1)} %slice_bitcast_fusion.4), channel_id=1, source_target_pairs={{0,1},{1,0},{2,3},{3,2},{4,5},{5,4},{6,7},{7,6},{8,9},{9,8},{10,11... | collective-permute-start | bytes 2359304 | tf_op jit(solution)/shard_map/ppermute | solution.py:16
  217.0 19.9 %collective-permute-start.4 = (bf16[4,48,2048]{2,1,0:T(8,128)(2,1)S(1)}, bf16[4,48,2048]{2,1,0:T(8,128)(2,1)S(1)}, u32[]{:S(2)}, u32[]{:S(2)}) collective-permute-start(bf16[4,48,2048]{2,1,0:T(8,128)(2,1)S(1)} %slice_bitcast_fusion.6), channel_id=1, source_target_pairs={{0,1},{1,0},{2,3},{3,2},{4,5},{5,4},{6,7},{7,6},{8,9},{9,8},{10,11... | collective-permute-start | bytes 2359304 | tf_op jit(solution)/shard_map/ppermute | solution.py:16
  219.6 12.6 %collective-permute-start.33 = (bf16[4,48,2048]{2,1,0:T(8,128)(2,1)S(1)}, bf16[4,48,2048]{2,1,0:T(8,128)(2,1)S(1)}, u32[]{:S(2)}, u32[]{:S(2)}) collective-permute-start(bf16[4,48,2048]{2,1,0:T(8,128)(2,1)S(1)} %slice_bitcast_fusion), channel_id=1, source_target_pairs={{0,1},{1,0},{2,3},{3,2},{4,5},{5,4},{6,7},{7,6},{8,9},{9,8},{10,11... | collective-permute-start | bytes 2359304 | tf_op jit(solution)/shard_map/ppermute | solution.py:16
  231.5 25.5 %collective-permute-start.25 = (bf16[48,2048]{1,0:T(8,128)(2,1)S(1)}, bf16[48,2048]{1,0:T(8,128)(2,1)S(1)}, u32[]{:S(2)}, u32[]{:S(2)}) collective-permute-start(bf16[48,2048]{1,0:T(8,128)(2,1)S(1)} %get-tuple-element.66), channel_id=1, source_target_pairs={{0,4},{1,5},{2,6},{3,7},{4,0},{5,1},{6,2},{7,3},{8,12},{9,13},{10,... | collective-permute-start | bytes 589832 | tf_op jit(solution)/shard_map/ppermute | solution.py:16
  232.2 25.6 %collective-permute-start.26 = (bf16[48,2048]{1,0:T(8,128)(2,1)S(1)}, bf16[48,2048]{1,0:T(8,128)(2,1)S(1)}, u32[]{:S(2)}, u32[]{:S(2)}) collective-permute-start(bf16[48,2048]{1,0:T(8,128)(2,1)S(1)} %get-tuple-element.65), channel_id=1, source_target_pairs={{0,6},{1,7},{2,4},{3,5},{4,2},{5,3},{6,0},{7,1},{8,14},{9,15},{10,... | collective-permute-start | bytes 589832 | tf_op jit(solution)/shard_map/ppermute | solution.py:16
  234.0 12.3 %collective-permute-start.34 = (bf16[48,2048]{1,0:T(8,128)(2,1)S(1)}, bf16[48,2048]{1,0:T(8,128)(2,1)S(1)}, u32[]{:S(2)}, u32[]{:S(2)}) collective-permute-start(bf16[48,2048]{1,0:T(8,128)(2,1)S(1)} %get-tuple-element.79), channel_id=1, source_target_pairs={{0,2},{1,3},{2,0},{3,1},{4,6},{5,7},{6,4},{7,5},{8,10},{9,11},{10,... | collective-permute-start | bytes 589832 | tf_op jit(solution)/shard_map/ppermute | solution.py:16
  238.0 21.3 %collective-permute-start.14 = (bf16[48,2048]{1,0:T(8,128)(2,1)S(1)}, bf16[48,2048]{1,0:T(8,128)(2,1)S(1)}, u32[]{:S(2)}, u32[]{:S(2)}) collective-permute-start(bf16[48,2048]{1,0:T(8,128)(2,1)S(1)} %get-tuple-element.71), channel_id=1, source_target_pairs={{0,2},{1,3},{2,0},{3,1},{4,6},{5,7},{6,4},{7,5},{8,10},{9,11},{10,... | collective-permute-start | bytes 589832 | tf_op jit(solution)/shard_map/ppermute | solution.py:16
  246.3 14.3 %collective-permute-start.15 = (bf16[48,2048]{1,0:T(8,128)(2,1)S(1)}, bf16[48,2048]{1,0:T(8,128)(2,1)S(1)}, u32[]{:S(2)}, u32[]{:S(2)}) collective-permute-start(bf16[48,2048]{1,0:T(8,128)(2,1)S(1)} %get-tuple-element.70), channel_id=1, source_target_pairs={{0,4},{1,5},{2,6},{3,7},{4,0},{5,1},{6,2},{7,3},{8,12},{9,13},{10,... | collective-permute-start | bytes 589832 | tf_op jit(solution)/shard_map/ppermute | solution.py:16
  259.3 11.0 %collective-permute-start.7 = (bf16[48,2048]{1,0:T(8,128)(2,1)S(1)}, bf16[48,2048]{1,0:T(8,128)(2,1)S(1)}, u32[]{:S(2)}, u32[]{:S(2)}) collective-permute-start(bf16[48,2048]{1,0:T(8,128)(2,1)S(1)} %get-tuple-element.73), channel_id=1, source_target_pairs={{0,6},{1,7},{2,4},{3,5},{4,2},{5,3},{6,0},{7,1},{8,14},{9,15},{10,... | collective-permute-start | bytes 589832 | tf_op jit(solution)/shard_map/ppermute | solution.py:16
  260.6 13.9 %collective-permute-start.37 = (bf16[96,2048]{1,0:T(8,128)(2,1)S(1)}, bf16[96,2048]{1,0:T(8,128)(2,1)S(1)}, u32[]{:S(2)}, u32[]{:S(2)}) collective-permute-start(bf16[96,2048]{1,0:T(8,128)(2,1)S(1)} %convolution_convert_fusion.18), channel_id=1, source_target_pairs={{0,24},{8,16},{16,8},{24,0},{1,25},{9,17},{17,9},{25,1},{2,26},{10... | collective-permute-start | bytes 1179656 | tf_op jit(solution)/shard_map/ppermute | solution.py:16
  264.1 29.9 %collective-permute-start.27 = (bf16[96,2048]{1,0:T(8,128)(2,1)}, bf16[96,2048]{1,0:T(8,128)(2,1)}, u32[]{:S(2)}, u32[]{:S(2)}) collective-permute-start(bf16[96,2048]{1,0:T(8,128)(2,1)} %convolution_convert_fusion.19), channel_id=1, source_target_pairs={{0,16},{8,24},{16,0},{24,8},{1,17},{9,25},{17,1},{25,9},{2,18},{10... | collective-permute-start | bytes 1179656 | tf_op jit(solution)/shard_map/ppermute | solution.py:16
  267.2 18.8 %collective-permute-start.17 = (bf16[96,2048]{1,0:T(8,128)(2,1)S(1)}, bf16[96,2048]{1,0:T(8,128)(2,1)S(1)}, u32[]{:S(2)}, u32[]{:S(2)}) collective-permute-start(bf16[96,2048]{1,0:T(8,128)(2,1)S(1)} %convolution_convert_fusion.20), channel_id=1, source_target_pairs={{0,8},{8,0},{16,24},{24,16},{1,9},{9,1},{17,25},{25,17},{2,10},{10... | collective-permute-start | bytes 1179656 | tf_op jit(solution)/shard_map/ppermute | solution.py:16
  (43 other events, 383.0 us)

commit v2 on v1

--- a/solution.py
+++ b/solution.py
@@ -1,12 +1,18 @@
+import functools
+
 import jax
 import jax.numpy as jnp
 from jax import lax
+from jax.experimental import pallas as pl
+from jax.experimental.pallas import tpu as pltpu
 from jax.sharding import PartitionSpec as P
 
 BF = jnp.bfloat16
 F32 = jnp.float32
 ACROSS = (((0,), (0,)), ((), ()))
 INNER = (((1,), (1,)), ((), ()))
+MESH = pl.DeviceIdType.MESH
+VMEM_BYTES = 61 * 1024 * 1024
 
 
 def swap(value, axis, shift):
@@ -28,7 +34,7 @@
     return picked, rank, gate
 
 
-def local(tokens, out_grad, expert_ids, gates, w_gate, w_up, w_down, gate_saved, up_saved):
+def local_permutes(tokens, out_grad, expert_ids, gates, w_gate, w_up, w_down, gate_saved, up_saved):
     n_wide = lax.axis_size("wide")
     n_narrow = lax.axis_size("narrow")
     devices = n_wide * n_narrow
@@ -133,6 +139,349 @@
     return (token_grad.astype(BF), grad_gate[None], grad_up[None], grad_down[None])
 
 
+def exchange_kernel(
+    n_wide, n_narrow, cap, tokens_ref, grad_ref, pack_ref, spread_ref, info_ref, wg_hbm, wu_hbm,
+    wd_hbm, gate_hbm, up_hbm, out_ref, x_hbm, dy_hbm, gg_hbm, ug_hbm, send, zbuf, stage_x, stage_dy,
+    dy_rows, w_gate, w_up, w_down, gate_in, up_in, gg, ug, part, half_in, back, pick_out, pick_in,
+    load_sem, keep_sem, save_sem, z_sem, px_sem, pd_sem, sx_sem, sd_sem, half_sem, back_sem, zb_sem,
+):
+    spots = n_narrow // 2
+    width = tokens_ref.shape[1]
+    rows = pack_ref.shape[1]
+    slots = spots * cap
+    chunk = n_narrow * cap
+    mz = lax.axis_index("wide")
+    mn = lax.axis_index("narrow")
+    ms = mn // 2
+    core = mn - 2 * ms
+    sibling = ms * 2 + (1 - core)
+
+    def plane_id(q):
+        return (ms ^ q) * 2 + core
+
+    def remote(src, dst, sems, wide, narrow):
+        copy = pltpu.make_async_remote_copy(
+            src_ref=src, dst_ref=dst, send_sem=sems[0], recv_sem=sems[1],
+            device_id=(wide, narrow), device_id_type=MESH,
+        )
+        copy.start()
+        return copy
+
+    def pair(sem, *index):
+        return sem.at[(0, *index)], sem.at[(1, *index)]
+
+    def here(src, dst, sem):
+        copy = pltpu.make_async_copy(src, dst, sem)
+        copy.start()
+        return copy
+
+    loads = [
+        here(wd_hbm.at[0], w_down, load_sem.at[0]),
+        here(wg_hbm.at[0], w_gate, load_sem.at[1]),
+        here(wu_hbm.at[0], w_up, load_sem.at[2]),
+    ]
+    saved = []
+    for k in range(n_wide):
+        source = pl.ds((mz ^ k) * chunk, chunk)
+        saved.append((
+            here(gate_hbm.at[0, source], gate_in.at[k], load_sem.at[3 + 2 * k]),
+            here(up_hbm.at[0, source], up_in.at[k], load_sem.at[4 + 2 * k]),
+        ))
+
+    barrier = pltpu.get_barrier_semaphore()
+    for k in range(1, n_wide):
+        pl.semaphore_signal(barrier, inc=1, device_id=(mz ^ k, mn), device_id_type=MESH)
+    for q in range(1, spots):
+        pl.semaphore_signal(barrier, inc=1, device_id=(mz, plane_id(q)), device_id_type=MESH)
+    pl.semaphore_signal(barrier, inc=1, device_id=(mz, sibling), device_id_type=MESH)
+
+    def pack(k):
+        send[k, :, :width] = jnp.dot(
+            pack_ref[k], tokens_ref[...], preferred_element_type=F32
+        ).astype(BF)
+        send[k, :, width : 2 * width] = jnp.dot(
+            pack_ref[k], grad_ref[...], preferred_element_type=F32
+        ).astype(BF)
+        send[k, :, 2 * width :] = info_ref[k]
+
+    z_copies = [None] * n_wide
+    for k in list(range(1, n_wide)) + [0]:
+        pack(k)
+        if k == 1:
+            pl.semaphore_wait(barrier, n_wide - 1 + spots - 1 + 1)
+        if k:
+            z_copies[k] = remote(send.at[k], zbuf.at[k], pair(z_sem, k), mz ^ k, mn)
+
+    ended, kept = [], []
+    plane, shared = {}, {}
+
+    def make_slots(k):
+        if k:
+            z_copies[k].wait_recv()
+        got = zbuf if k else send
+        info = jnp.transpose(got[k, :, 2 * width :].astype(F32))
+        line = lax.broadcasted_iota(jnp.int32, (slots, rows), 0)
+        rank = jnp.zeros((slots, rows), F32)
+        gate = jnp.zeros((slots, rows), F32)
+        rest = line
+        for e in range(spots):
+            inside = (line >= e * cap) & (line < (e + 1) * cap)
+            rank = jnp.where(inside, info[e : e + 1, :], rank)
+            gate = jnp.where(inside, info[spots + e : spots + e + 1, :], gate)
+            rest = jnp.where(inside, line - e * cap, rest)
+        hit = rank == rest.astype(F32)
+        table = jnp.where(hit, 1.0, 0.0).astype(BF)
+        scaled = jnp.where(hit, gate, 0.0).astype(BF)
+        stage_dy[k] = jnp.dot(
+            scaled, got[k, :, width : 2 * width], preferred_element_type=F32
+        ).astype(BF).reshape(spots, cap, width)
+        for q in range(1, spots):
+            to = (mz ^ k) * n_narrow + mn
+            plane[k, q, 1] = remote(
+                stage_dy.at[k, ms ^ q], dy_rows.at[to], pair(pd_sem, k, q), mz, plane_id(q)
+            )
+        stage_x[k] = jnp.dot(
+            table, got[k, :, :width], preferred_element_type=F32
+        ).astype(BF).reshape(spots, cap, width)
+        for q in range(1, spots):
+            to = (mz ^ k) * n_narrow + mn
+            plane[k, q, 0] = remote(
+                stage_x.at[k, ms ^ q], x_hbm.at[to], pair(px_sem, k, q), mz, plane_id(q)
+            )
+        to = (mz ^ k) * n_narrow + mn
+        kept.append((
+            here(stage_dy.at[k, ms], dy_rows.at[to], keep_sem.at[k, 0]),
+            here(stage_x.at[k, ms], x_hbm.at[to], keep_sem.at[k, 1]),
+        ))
+        shared[k, 0, 1] = remote(
+            stage_dy.at[k, ms], dy_rows.at[to], pair(sd_sem, k, 0), mz, sibling
+        )
+        shared[k, 0, 0] = remote(stage_x.at[k, ms], x_hbm.at[to], pair(sx_sem, k, 0), mz, sibling)
+
+    def share(k):
+        for which, rows_ref, sem in ((1, dy_rows, sd_sem), (0, x_hbm, sx_sem)):
+            for q in range(1, spots):
+                plane[k, q, which].wait_recv()
+                at = (mz ^ k) * n_narrow + plane_id(q)
+                shared[k, q, which] = remote(
+                    rows_ref.at[at], rows_ref.at[at], pair(sem, k, q), mz, sibling
+                )
+
+    halves = [None] * n_wide
+    saves = []
+
+    def expert(k):
+        kept[k][0].wait()
+        for q in range(spots):
+            shared[k, q, 1].wait_recv()
+        if k == 0:
+            loads[0].wait()
+        for copy in saved[k]:
+            copy.wait()
+        source = pl.ds((mz ^ k) * n_narrow, n_narrow)
+        dy = dy_rows[source].reshape(chunk, width)
+        act_grad = lax.dot_general(dy, w_down[...], INNER, preferred_element_type=F32)
+        gate_pre = gate_in[k].astype(F32)
+        up_pre = up_in[k].astype(F32)
+        sigma = jax.nn.sigmoid(gate_pre)
+        ug[k] = (act_grad * (gate_pre * sigma)).astype(BF)
+        gg[k] = (act_grad * up_pre * sigma * (1.0 + gate_pre * (1.0 - sigma))).astype(BF)
+        source_rows = pl.ds((mz ^ k) * chunk, chunk)
+        saves.append(here(gg.at[k], gg_hbm.at[source_rows], save_sem.at[k, 0]))
+        saves.append(here(ug.at[k], ug_hbm.at[source_rows], save_sem.at[k, 1]))
+        saves.append(here(dy_rows.at[source], dy_hbm.at[source], save_sem.at[k, 2]))
+        if k == 0:
+            loads[1].wait()
+            loads[2].wait()
+        tile = 512
+
+        def columns(j, carry):
+            at = pl.ds(pl.multiple_of(j * tile, tile), tile)
+            value = lax.dot_general(gg[k], w_gate[at, :], INNER, preferred_element_type=F32)
+            value = value + lax.dot_general(ug[k], w_up[at, :], INNER, preferred_element_type=F32)
+            value = value.astype(BF).reshape(spots, 2, cap, tile)
+            for c in range(2):
+                part[k, c, :, :, at] = value[:, c]
+            return carry
+
+        lax.fori_loop(0, width // tile, columns, 0)
+        halves[k] = remote(part.at[k, 1 - core], half_in.at[k], pair(half_sem, k), mz, sibling)
+
+    returned = {}
+
+    def give_back(k):
+        halves[k].wait_recv()
+        whole = part[k, core].astype(F32) + half_in[k].astype(F32)
+        part[k, core] = whole.astype(BF)
+        for q in range(1, spots):
+            returned[k, q] = remote(
+                part.at[k, core, ms ^ q], back.at[k, ms], pair(back_sem, k, q), mz, plane_id(q)
+            )
+        returned[k, 0] = here(part.at[k, core, ms], back.at[k, ms], keep_sem.at[k, 2])
+
+    z_back = [None] * n_wide
+
+    def pick(k):
+        for q in range(1, spots):
+            returned[k, q].wait_recv()
+        returned[k, 0].wait()
+        got = zbuf if k else send
+        info = got[k, :, 2 * width :].astype(F32)
+        line = lax.broadcasted_iota(jnp.int32, (rows, slots), 1)
+        rank = jnp.zeros((rows, slots), F32)
+        rest = line
+        for e in range(spots):
+            inside = (line >= e * cap) & (line < (e + 1) * cap)
+            rank = jnp.where(inside, info[:, e : e + 1], rank)
+            rest = jnp.where(inside, line - e * cap, rest)
+        table = jnp.where(rank == rest.astype(F32), 1.0, 0.0).astype(BF)
+        value = jnp.dot(table, back[k].reshape(slots, width), preferred_element_type=F32)
+        pick_out[k] = value.astype(BF)
+        if k:
+            z_back[k] = remote(pick_out.at[k], pick_in.at[k], pair(zb_sem, k), mz ^ k, mn)
+
+    last = n_wide - 1
+    for k in range(n_wide + 4):
+        if k <= last:
+            make_slots(k)
+        if 1 <= k <= last + 1:
+            expert(k - 1)
+        if 3 <= k <= last + 3:
+            pick(k - 3)
+        if k <= last:
+            share(k)
+        if 2 <= k <= last + 2:
+            give_back(k - 2)
+
+    total = jnp.dot(spread_ref[0], pick_out[0], preferred_element_type=F32)
+    for k in range(1, n_wide):
+        z_back[k].wait_recv()
+        total = total + jnp.dot(spread_ref[k], pick_in[k], preferred_element_type=F32)
+    out_ref[...] = total.astype(BF)
+
+    for k in range(n_wide):
+        kept[k][1].wait()
+        for q in range(spots):
+            shared[k, q, 0].wait_recv()
+            shared[k, q, 0].wait_send()
+            shared[k, q, 1].wait_send()
+            if q:
+                plane[k, q, 0].wait_send()
+                plane[k, q, 1].wait_send()
+                returned[k, q].wait_send()
+        halves[k].wait_send()
+        if k:
+            z_copies[k].wait_send()
+            z_back[k].wait_send()
+    for copy in saves:
+        copy.wait()
+
+
+def exchange(tokens, out_grad, pack, spread, info, w_gate, w_up, w_down, gate_saved, up_saved):
+    n_wide, n_narrow = lax.axis_size("wide"), lax.axis_size("narrow")
+    devices = n_wide * n_narrow
+    spots = n_narrow // 2
+    count, width = tokens.shape
+    rows = pack.shape[1]
+    half = w_gate.shape[2]
+    cap = gate_saved.shape[1] // devices
+    chunk = n_narrow * cap
+    wide_row = 2 * width + info.shape[2]
+    flops = 6 * devices * cap * width * half
+    vmem = pl.BlockSpec(memory_space=pltpu.VMEM)
+    hbm = pl.BlockSpec(memory_space=pl.ANY)
+    sem = pltpu.SemaphoreType.DMA
+    return pl.pallas_call(
+        functools.partial(exchange_kernel, n_wide, n_narrow, cap),
+        out_shape=(
+            jax.ShapeDtypeStruct((count, width), BF),
+            jax.ShapeDtypeStruct((devices, cap, width), BF),
+            jax.ShapeDtypeStruct((devices, cap, width), BF),
+            jax.ShapeDtypeStruct((devices * cap, half), BF),
+            jax.ShapeDtypeStruct((devices * cap, half), BF),
+        ),
+        in_specs=[vmem] * 5 + [hbm] * 5,
+        out_specs=(vmem, hbm, hbm, hbm, hbm),
+        scratch_shapes=[
+            pltpu.VMEM((n_wide, rows, wide_row), BF),
+            pltpu.VMEM((n_wide, rows, wide_row), BF),
+            pltpu.VMEM((n_wide, spots, cap, width), BF),
+            pltpu.VMEM((n_wide, spots, cap, width), BF),
+            pltpu.VMEM((devices, cap, width), BF),
+            pltpu.VMEM((width, half), BF),
+            pltpu.VMEM((width, half), BF),
+            pltpu.VMEM((half, width), BF),
+            pltpu.VMEM((n_wide, chunk, half), BF),
+            pltpu.VMEM((n_wide, chunk, half), BF),
+            pltpu.VMEM((n_wide, chunk, half), BF),
+            pltpu.VMEM((n_wide, chunk, half), BF),
+            pltpu.VMEM((n_wide, 2, spots, cap, width), BF),
+            pltpu.VMEM((n_wide, spots, cap, width), BF),
+            pltpu.VMEM((n_wide, spots, cap, width), BF),
+            pltpu.VMEM((n_wide, rows, width), BF),
+            pltpu.VMEM((n_wide, rows, width), BF),
+            sem((3 + 2 * n_wide,)),
+            sem((n_wide, 3)),
+            sem((n_wide, 3)),
+            sem((2, n_wide)),
+            sem((2, n_wide, spots)),
+            sem((2, n_wide, spots)),
+            sem((2, n_wide, spots)),
+            sem((2, n_wide, spots)),
+            sem((2, n_wide)),
+            sem((2, n_wide, spots)),
+            sem((2, n_wide)),
+        ],
+        compiler_params=pltpu.CompilerParams(
+            collective_id=0, has_side_effects=True, vmem_limit_bytes=VMEM_BYTES
+        ),
+        cost_estimate=pl.CostEstimate(flops=flops, bytes_accessed=40_000_000, transcendentals=0),
+    )(tokens, out_grad, pack, spread, info, w_gate, w_up, w_down, gate_saved, up_saved)
+
+
+def local_kernel(tokens, out_grad, expert_ids, gates, w_gate, w_up, w_down, gate_saved, up_saved):
+    n_wide = lax.axis_size("wide")
+    n_narrow = lax.axis_size("narrow")
+    devices = n_wide * n_narrow
+    experts = devices // 2
+    spots = n_narrow // 2
+    count, width = tokens.shape
+    cap = gate_saved.shape[1] // devices
+    rows = count * (expert_ids.shape[1] // 2) // n_wide
+    picked, rank, gate = route_tables(expert_ids, gates, experts, cap)
+    groups = lax.axis_index("wide") ^ jnp.arange(n_wide, dtype=jnp.int32)
+    member = jnp.any(picked.reshape(count, n_wide, spots), axis=2)
+    row = lax.broadcasted_iota(jnp.int32, (count, count), 0)
+    col = lax.broadcasted_iota(jnp.int32, (count, count), 1)
+    place = jnp.dot((col < row).astype(BF), member.astype(BF), preferred_element_type=F32)
+    place = jnp.take(jnp.where(member, place, -1.0), groups, axis=1).T
+    number = jnp.arange(rows, dtype=F32)
+    spread = (place[:, :, None] == number[None, None, :]).astype(BF)
+    pack = (place[:, None, :] == number[None, :, None]).astype(BF)
+    info = jnp.concatenate([rank.reshape(count, n_wide, spots), gate.reshape(count, n_wide, spots)], 2)
+    info = jnp.take(info, groups, axis=1).astype(BF).transpose(1, 0, 2)
+    info = jnp.pad(info, ((0, 0), (0, 0), (0, 128 - 2 * spots)))
+    info = jnp.einsum("krt,ktc->krc", pack, info, preferred_element_type=F32).astype(BF)
+    token_grad, rows_x, rows_dy, gate_grad, up_grad = exchange(
+        tokens, out_grad, pack, spread, info, w_gate, w_up, w_down, gate_saved, up_saved
+    )
+    rows_x = rows_x.reshape(devices * cap, width)
+    rows_dy = rows_dy.reshape(devices * cap, width)
+    act = (jax.nn.silu(gate_saved[0].astype(F32)) * up_saved[0].astype(F32)).astype(BF)
+    grad_gate = lax.dot_general(rows_x, gate_grad, ACROSS, preferred_element_type=F32).astype(BF)
+    grad_up = lax.dot_general(rows_x, up_grad, ACROSS, preferred_element_type=F32).astype(BF)
+    grad_down = lax.dot_general(act, rows_dy, ACROSS, preferred_element_type=F32).astype(BF)
+    return (token_grad, grad_gate[None], grad_up[None], grad_down[None])
+
+
+def local(tokens, out_grad, expert_ids, gates, w_gate, w_up, w_down, gate_saved, up_saved):
+    slots = gate_saved.shape[1]
+    cap = slots // (lax.axis_size("wide") * lax.axis_size("narrow"))
+    fits = 8 * slots * tokens.shape[1] <= VMEM_BYTES and cap % 16 == 0
+    body = local_kernel if fits else local_permutes
+    return body(tokens, out_grad, expert_ids, gates, w_gate, w_up, w_down, gate_saved, up_saved)
+
+
 def solution(mesh):
     row = P(("wide", "narrow"), None)
     slab = P(("wide", "narrow"), None, None)

time: 301 us -> 195 us (0.65)
  Pallas kernels: 0 us -> 146 us
  waiting for transfers between devices: 80.7 us -> 0 us
  matrix products: 74.9 us -> 23.7 us
  starting transfers between devices: 40.1 us -> 0 us
  other arithmetic: 42.5 us -> 3.77 us
  local copies, waits for them, and re-layouts: 56.7 us -> 18 us
    pallas_call x0 -> x1, Pallas kernels: none -> 146 us  [exchange(): pl.pallas_call(functools.partial(exchange_kernel, n_wide, n_narrow, cap),...]
    ppermute x38 -> x0, waiting for transfers between devices: 80.7 us -> none  [swap(): return lax.ppermute(value, axis, [(i, i ^ shift) for i in range(size)])]
    dot_general x41 -> x5, matrix products: 74.7 us -> 23.5 us  [the longest x1 9.91 us: local_kernel(): lax.dot_general(rows_x, up_grad, ACROSS, preferred_element_type=F32)]
    ppermute x38 -> x0, starting transfers between devices: 40.1 us -> none  [swap(): return lax.ppermute(value, axis, [(i, i ^ shift) for i in range(size)])]
    convert_element_type x8 -> x0, local copies, waits for them, and re-layouts: 21 us -> none  [the longest x4 10.6 us: local(): gate_pre = gate_rows[step].astype(F32)]
    convert_element_type x13 -> x3, other arithmetic: 19.7 us -> 1.54 us  [the longest x1 0.79 us: local_kernel(): spread = (place[:, :, None] == number[None, None, :]).astype(BF)]
    gather x12 -> x2, local copies, waits for them, and re-layouts: 13.3 us -> 1.14 us  [the longest x1 0.58 us: local_kernel(): place = jnp.take(jnp.where(member, place, -1.0), groups, axis=1).T]
    another operation x8 -> x0, other arithmetic: 7.99 us -> none  [the longest x4 4.54 us: local(): chip = jnp.stack([plane, swap(plane, 'narrow', 1)], 1)]
  transfers between devices with their start and end apart: 38 -> 0, of which waited for: 19 -> 0; matrix products, arithmetic and copies ran while one was open for 51% -> 0% of each run, Pallas kernels for 0% -> 0%
where the time goes in v2:
time: 195 us; the launch traced here: 192 us
  Pallas kernels  146 us (75%)
  matrix products  23.7 us (12%)
  local copies, waits for them, and re-layouts  18 us (9%)
  other arithmetic  3.77 us (2%)
    pallas_call x1, Pallas kernels, exchange(): pl.pallas_call(functools.partial(exchange_kernel, n_wide, n_narrow, cap),...  146 us
    unnamed x21, local copies, waits for them, and re-layouts  16.8 us
    dot_general x1, matrix products, local_kernel(): lax.dot_general(rows_x, up_grad, ACROSS, preferred_element_type=F32)  9.91 us
    dot_general x1, matrix products, local_kernel(): lax.dot_general(act, rows_dy, ACROSS, preferred_element_type=F32).astype(BF)  6.47 us
    dot_general x1, matrix products, local_kernel(): lax.dot_general(rows_x, gate_grad, ACROSS, preferred_element_type=F32)  6.21 us

profile of v2, /device:TPU:0, one launch (start us, length us, event | category | flops | bytes accessed | tf_op | source)
XLA Modules:
  0.0 192.4 jit_solution(4928087832795710771)
XLA Ops:
  0.7 0.7 fusion.15
  1.4 0.1 convolution_select_fusion
  1.5 0.6 gather_fusion
  2.1 0.1 broadcast_select_fusion
  2.2 0.1 and_select_fusion
  2.3 0.7 convert_element_type.50
  3.0 0.7 select_reduce_fusion
  3.7 0.6 gather_fusion.1
  4.3 0.1 select_convert_fusion
  4.4 0.8 convolution_convert_fusion.3.info_ref
  5.2 0.7 fusion.11.pack_ref
  5.9 0.8 fusion.10.spread_ref
  6.7 4.2 %copy.38.gate_hbm = bf16[1,1536,704]{2,1,0:T(8,128)(2,1)} copy(bf16[1,1536,704]{1,2,0:T(8,128)(2,1)} %param.16) | data formatting | bytes 4325376 | tf_op args[7]
  10.8 4.3 %copy.39.up_hbm = bf16[1,1536,704]{2,1,0:T(8,128)(2,1)} copy(bf16[1,1536,704]{1,2,0:T(8,128)(2,1)} %param.17) | data formatting | bytes 4325376 | tf_op args[8]
  15.2 0.0 copy-done
  15.2 2.9 %copy.36.wg_hbm = bf16[1,2048,704]{2,1,0:T(8,128)(2,1)} copy(bf16[1,2048,704]{1,2,0:T(8,128)(2,1)S(1)} %copy-done) | data formatting | bytes 5767168 | tf_op args[4]
  18.0 4.7 %copy.37.wu_hbm = bf16[1,2048,704]{2,1,0:T(8,128)(2,1)} copy(bf16[1,2048,704]{1,2,0:T(8,128)(2,1)} %param.14) | data formatting | bytes 5767168 | tf_op args[5]
  22.7 146.2 %shard_map.120 = (bf16[128,2048]{1,0:T(8,128)(2,1)}, bf16[32,48,2048]{2,1,0:T(8,128)(2,1)}, bf16[32,48,2048]{2,1,0:T(8,128)(2,1)}, bf16[1536,704]{1,0:T(8,128)(2,1)}, bf16[1536,704]{1,0:T(8,128)(2,1)}) custom-call(bf16[128,2048]{1,0:T(8,128)(2,1)} %tokens_ref.1, bf16[128,2048]{1,0:T(8,128)(2,1)} %grad_ref.1, bf16[4,96,128]{2,1,0:T(8,128)(2,1)} %fusion.11.pack_ref, ...), custom_call_target="tpu_custom_call" | custom-call | flops 13287555072 | bytes 40000000 | tf_op jit(solution)/shard_map/pallas_call | solution.py:394
  168.9 0.0 copy-start.4
  168.9 0.0 copy-start.5
  168.9 0.0 slice-start
  168.9 9.9 %fusion.6 = bf16[1,2048,704]{1,2,0:T(8,128)(2,1)} fusion(bf16[1536,2048]{1,0:T(8,128)(2,1)} %bitcast.29, bf16[1536,704]{1,0:T(8,128)(2,1)} %get-tuple-element.12), kind=kOutput, calls=%fused_computation.13 | convolution fusion | flops 4430626816 | bytes 11337728 | tf_op jit(solution)/shard_map/dot_general | solution.py:472
  178.8 0.0 copy-done.4
  178.8 0.0 copy-done.5
  178.8 0.0 copy-start.2
  178.8 0.0 slice-start.1
  178.8 6.2 %fusion.5 = bf16[1,2048,704]{1,2,0:T(8,128)(2,1)} fusion(bf16[1536,2048]{1,0:T(8,128)(2,1)S(1)} %bitcast.30, bf16[1536,704]{1,0:T(8,128)(2,1)S(1)} %copy-done.5), kind=kOutput, calls=%fused_computation.12 | convolution fusion | flops 4430626816 | bytes 11337728 | tf_op jit(solution)/shard_map/dot_general | solution.py:471
  185.1 0.0 slice-done
  185.1 0.0 copy-done.1
  185.1 0.0 copy-done.2
  185.1 6.5 %fusion.7 = bf16[1,704,2048]{2,1,0:T(8,128)(2,1)} fusion(bf16[1536,2048]{1,0:T(8,128)(2,1)S(1)} %bitcast.28, bf16[1,1536,704]{1,2,0:T(8,128)(2,1)S(1)} %copy-done.2, bf16[1,1536,704]{1,2,0:T(8,128)(2,1)S(1)} %copy-done.1), kind=kOutput, calls=%fused_computation.14 | convolution fusion | flops 4439277568 | bytes 13500416 | tf_op jit(solution)/shard_map/dot_general | solution.py:473
  191.6 0.8 copy.42
  (11 shorter events, 0.1 us)
Async XLA Ops:
  10.8 4.3 %copy-start = (bf16[1,2048,704]{1,2,0:T(8,128)(2,1)S(1)}, bf16[1,2048,704]{1,2,0:T(8,128)(2,1)}, u32[]{:S(2)}) copy-start(bf16[1,2048,704]{1,2,0:T(8,128)(2,1)} %param.13) | copy-start | bytes 8650756
  168.9 9.9 %copy-start.4 = (bf16[32,48,2048]{2,1,0:T(8,128)(2,1)S(1)}, bf16[32,48,2048]{2,1,0:T(8,128)(2,1)}, u32[]{:S(2)}) copy-start(bf16[32,48,2048]{2,1,0:T(8,128)(2,1)} %get-tuple-element.10) | copy-start | bytes 18874372
  168.9 9.9 %copy-start.5 = (bf16[1536,704]{1,0:T(8,128)(2,1)S(1)}, bf16[1536,704]{1,0:T(8,128)(2,1)}, u32[]{:S(2)}) copy-start(bf16[1536,704]{1,0:T(8,128)(2,1)} %get-tuple-element.11) | copy-start | bytes 6488068
  168.9 16.2 %slice-start = ((s8[6291456]{0:T(1024)(128)(4,1)}), s8[4194304]{0:T(1024)(128)(4,1)S(1)}, s32[]{:S(2)}) async-start(s8[6291456]{0:T(1024)(128)(4,1)} %bitcast.26), calls=%async_computation | async-start | bytes 8388608
  178.8 6.2 %copy-start.1 = (bf16[1,1536,704]{1,2,0:T(8,128)(2,1)S(1)}, bf16[1,1536,704]{1,2,0:T(8,128)(2,1)}, u32[]{:S(2)}) copy-start(bf16[1,1536,704]{1,2,0:T(8,128)(2,1)} %param.16) | copy-start | bytes 6488068
  178.8 6.2 %copy-start.2 = (bf16[1,1536,704]{1,2,0:T(8,128)(2,1)S(1)}, bf16[1,1536,704]{1,2,0:T(8,128)(2,1)}, u32[]{:S(2)}) copy-start(bf16[1,1536,704]{1,2,0:T(8,128)(2,1)} %param.17) | copy-start | bytes 6488068
  178.8 6.2 %slice-start.1 = ((s8[6291456]{0:T(1024)(128)(4,1)}), s8[2097152]{0:T(1024)(128)(4,1)S(1)}, s32[]{:S(2)}) async-start(s8[6291456]{0:T(1024)(128)(4,1)} %bitcast.26), calls=%async_computation.1 | async-start | bytes 4194304
  185.1 6.5 %copy-start.3 = (bf16[128,2048]{1,0:T(8,128)(2,1)S(1)}, bf16[128,2048]{1,0:T(8,128)(2,1)}, u32[]{:S(2)}) copy-start(bf16[128,2048]{1,0:T(8,128)(2,1)} %get-tuple-element.18) | copy-start | bytes 1572868

commit v3 on v2

--- a/solution.py
+++ b/solution.py
@@ -141,9 +141,9 @@
 
 def exchange_kernel(
     n_wide, n_narrow, cap, tokens_ref, grad_ref, pack_ref, spread_ref, info_ref, wg_hbm, wu_hbm,
-    wd_hbm, gate_hbm, up_hbm, out_ref, x_hbm, dy_hbm, gg_hbm, ug_hbm, send, zbuf, stage_x, stage_dy,
-    dy_rows, w_gate, w_up, w_down, gate_in, up_in, gg, ug, part, half_in, back, pick_out, pick_in,
-    load_sem, keep_sem, save_sem, z_sem, px_sem, pd_sem, sx_sem, sd_sem, half_sem, back_sem, zb_sem,
+    wd_hbm, gate_hbm, up_hbm, out_ref, x_hbm, dy_hbm, gg_hbm, ug_hbm, send_x, send_dy, zx, zdy,
+    stage_x, stage_dy, dy_rows, w_gate, w_up, w_down, gate_in, up_in, gg, ug, gg_rows, ug_rows, part, half_in, back, pick_out, pick_in,
+    load_sem, keep_sem, save_sem, zx_sem, zdy_sem, px_sem, pd_sem, sx_sem, sd_sem, half_sem, back_sem, zb_sem,
 ):
     spots = n_narrow // 2
     width = tokens_ref.shape[1]
@@ -182,10 +182,10 @@
     ]
     saved = []
     for k in range(n_wide):
-        source = pl.ds((mz ^ k) * chunk, chunk)
+        source = pl.ds(pl.multiple_of((mz ^ k) * chunk, 128), chunk)
         saved.append((
-            here(gate_hbm.at[0, source], gate_in.at[k], load_sem.at[3 + 2 * k]),
-            here(up_hbm.at[0, source], up_in.at[k], load_sem.at[4 + 2 * k]),
+            here(gate_hbm.at[0, :, source], gate_in.at[k], load_sem.at[3 + 2 * k]),
+            here(up_hbm.at[0, :, source], up_in.at[k], load_sem.at[4 + 2 * k]),
         ))
 
     barrier = pltpu.get_barrier_semaphore()
@@ -195,31 +195,36 @@
         pl.semaphore_signal(barrier, inc=1, device_id=(mz, plane_id(q)), device_id_type=MESH)
     pl.semaphore_signal(barrier, inc=1, device_id=(mz, sibling), device_id_type=MESH)
 
-    def pack(k):
-        send[k, :, :width] = jnp.dot(
-            pack_ref[k], tokens_ref[...], preferred_element_type=F32
-        ).astype(BF)
-        send[k, :, width : 2 * width] = jnp.dot(
+    def pack_dy(k):
+        send_dy[k, :, :width] = jnp.dot(
             pack_ref[k], grad_ref[...], preferred_element_type=F32
         ).astype(BF)
-        send[k, :, 2 * width :] = info_ref[k]
-
-    z_copies = [None] * n_wide
-    for k in list(range(1, n_wide)) + [0]:
-        pack(k)
-        if k == 1:
-            pl.semaphore_wait(barrier, n_wide - 1 + spots - 1 + 1)
-        if k:
-            z_copies[k] = remote(send.at[k], zbuf.at[k], pair(z_sem, k), mz ^ k, mn)
-
-    ended, kept = [], []
+        send_dy[k, :, width:] = info_ref[k]
+
+    def pack_x(k):
+        send_x[k] = jnp.dot(pack_ref[k], tokens_ref[...], preferred_element_type=F32).astype(BF)
+
+    z_dy, z_x = [None] * n_wide, [None] * n_wide
+
+    def start_dy(k):
+        z_dy[k] = remote(send_dy.at[k], zdy.at[k], pair(zdy_sem, k), mz ^ k, mn)
+
+    def start_x(k):
+        z_x[k] = remote(send_x.at[k], zx.at[k], pair(zx_sem, k), mz ^ k, mn)
+
+    pack_dy(2)
+    pl.semaphore_wait(barrier, n_wide - 1 + spots - 1 + 1)
+    start_dy(2)
+    pack_dy(1)
+    start_dy(1)
+    pack_dy(0)
+
+    kept_dy, kept_x = {}, {}
     plane, shared = {}, {}
 
-    def make_slots(k):
-        if k:
-            z_copies[k].wait_recv()
-        got = zbuf if k else send
-        info = jnp.transpose(got[k, :, 2 * width :].astype(F32))
+    def tables(k):
+        got = zdy if k else send_dy
+        info = jnp.transpose(got[k, :, width:].astype(F32))
         line = lax.broadcasted_iota(jnp.int32, (slots, rows), 0)
         rank = jnp.zeros((slots, rows), F32)
         gate = jnp.zeros((slots, rows), F32)
@@ -229,49 +234,56 @@
             rank = jnp.where(inside, info[e : e + 1, :], rank)
             gate = jnp.where(inside, info[spots + e : spots + e + 1, :], gate)
             rest = jnp.where(inside, line - e * cap, rest)
-        hit = rank == rest.astype(F32)
-        table = jnp.where(hit, 1.0, 0.0).astype(BF)
+        return rank == rest.astype(F32), gate
+
+    def slots_dy(k):
+        if k:
+            z_dy[k].wait_recv()
+        got = zdy if k else send_dy
+        hit, gate = tables(k)
         scaled = jnp.where(hit, gate, 0.0).astype(BF)
-        stage_dy[k] = jnp.dot(
-            scaled, got[k, :, width : 2 * width], preferred_element_type=F32
-        ).astype(BF).reshape(spots, cap, width)
+        stage_dy[k] = jnp.dot(scaled, got[k, :, :width], preferred_element_type=F32).astype(
+            BF
+        ).reshape(spots, cap, width)
+        to = (mz ^ k) * n_narrow + mn
         for q in range(1, spots):
-            to = (mz ^ k) * n_narrow + mn
             plane[k, q, 1] = remote(
                 stage_dy.at[k, ms ^ q], dy_rows.at[to], pair(pd_sem, k, q), mz, plane_id(q)
             )
-        stage_x[k] = jnp.dot(
-            table, got[k, :, :width], preferred_element_type=F32
-        ).astype(BF).reshape(spots, cap, width)
+        kept_dy[k] = here(stage_dy.at[k, ms], dy_rows.at[to], keep_sem.at[k, 0])
+        shared[k, 0, 1] = remote(
+            stage_dy.at[k, ms], dy_rows.at[to], pair(sd_sem, k, 0), mz, sibling
+        )
+
+    def slots_x(k):
+        if k:
+            z_x[k].wait_recv()
+        got = zx if k else send_x
+        table = jnp.where(tables(k)[0], 1.0, 0.0).astype(BF)
+        stage_x[k] = jnp.dot(table, got[k], preferred_element_type=F32).astype(BF).reshape(
+            spots, cap, width
+        )
+        to = (mz ^ k) * n_narrow + mn
         for q in range(1, spots):
-            to = (mz ^ k) * n_narrow + mn
             plane[k, q, 0] = remote(
                 stage_x.at[k, ms ^ q], x_hbm.at[to], pair(px_sem, k, q), mz, plane_id(q)
             )
-        to = (mz ^ k) * n_narrow + mn
-        kept.append((
-            here(stage_dy.at[k, ms], dy_rows.at[to], keep_sem.at[k, 0]),
-            here(stage_x.at[k, ms], x_hbm.at[to], keep_sem.at[k, 1]),
-        ))
-        shared[k, 0, 1] = remote(
-            stage_dy.at[k, ms], dy_rows.at[to], pair(sd_sem, k, 0), mz, sibling
-        )
+        kept_x[k] = here(stage_x.at[k, ms], x_hbm.at[to], keep_sem.at[k, 1])
         shared[k, 0, 0] = remote(stage_x.at[k, ms], x_hbm.at[to], pair(sx_sem, k, 0), mz, sibling)
 
-    def share(k):
-        for which, rows_ref, sem in ((1, dy_rows, sd_sem), (0, x_hbm, sx_sem)):
-            for q in range(1, spots):
-                plane[k, q, which].wait_recv()
-                at = (mz ^ k) * n_narrow + plane_id(q)
-                shared[k, q, which] = remote(
-                    rows_ref.at[at], rows_ref.at[at], pair(sem, k, q), mz, sibling
-                )
+    def share(k, which, rows_ref, sem):
+        for q in range(1, spots):
+            plane[k, q, which].wait_recv()
+            at = (mz ^ k) * n_narrow + plane_id(q)
+            shared[k, q, which] = remote(
+                rows_ref.at[at], rows_ref.at[at], pair(sem, k, q), mz, sibling
+            )
 
     halves = [None] * n_wide
     saves = []
 
     def expert(k):
-        kept[k][0].wait()
+        kept_dy[k].wait()
         for q in range(spots):
             shared[k, q, 1].wait_recv()
         if k == 0:
@@ -280,15 +292,19 @@
             copy.wait()
         source = pl.ds((mz ^ k) * n_narrow, n_narrow)
         dy = dy_rows[source].reshape(chunk, width)
-        act_grad = lax.dot_general(dy, w_down[...], INNER, preferred_element_type=F32)
+        act_grad = lax.dot_general(w_down[...], dy, INNER, preferred_element_type=F32)
         gate_pre = gate_in[k].astype(F32)
         up_pre = up_in[k].astype(F32)
         sigma = jax.nn.sigmoid(gate_pre)
-        ug[k] = (act_grad * (gate_pre * sigma)).astype(BF)
-        gg[k] = (act_grad * up_pre * sigma * (1.0 + gate_pre * (1.0 - sigma))).astype(BF)
-        source_rows = pl.ds((mz ^ k) * chunk, chunk)
-        saves.append(here(gg.at[k], gg_hbm.at[source_rows], save_sem.at[k, 0]))
-        saves.append(here(ug.at[k], ug_hbm.at[source_rows], save_sem.at[k, 1]))
+        up_grad = act_grad * (gate_pre * sigma)
+        gate_grad = act_grad * up_pre * sigma * (1.0 + gate_pre * (1.0 - sigma))
+        ug[k] = up_grad.astype(BF)
+        gg[k] = gate_grad.astype(BF)
+        ug_rows[...] = jnp.transpose(ug[k])
+        gg_rows[...] = jnp.transpose(gg[k])
+        source_rows = pl.ds(pl.multiple_of((mz ^ k) * chunk, 128), chunk)
+        saves.append(here(gg.at[k], gg_hbm.at[:, source_rows], save_sem.at[k, 0]))
+        saves.append(here(ug.at[k], ug_hbm.at[:, source_rows], save_sem.at[k, 1]))
         saves.append(here(dy_rows.at[source], dy_hbm.at[source], save_sem.at[k, 2]))
         if k == 0:
             loads[1].wait()
@@ -297,8 +313,8 @@
 
         def columns(j, carry):
             at = pl.ds(pl.multiple_of(j * tile, tile), tile)
-            value = lax.dot_general(gg[k], w_gate[at, :], INNER, preferred_element_type=F32)
-            value = value + lax.dot_general(ug[k], w_up[at, :], INNER, preferred_element_type=F32)
+            value = jnp.dot(gg_rows[...], w_gate[:, at], preferred_element_type=F32)
+            value = value + jnp.dot(ug_rows[...], w_up[:, at], preferred_element_type=F32)
             value = value.astype(BF).reshape(spots, 2, cap, tile)
             for c in range(2):
                 part[k, c, :, :, at] = value[:, c]
@@ -325,8 +341,8 @@
         for q in range(1, spots):
             returned[k, q].wait_recv()
         returned[k, 0].wait()
-        got = zbuf if k else send
-        info = got[k, :, 2 * width :].astype(F32)
+        got = zdy if k else send_dy
+        info = got[k, :, width:].astype(F32)
         line = lax.broadcasted_iota(jnp.int32, (rows, slots), 1)
         rank = jnp.zeros((rows, slots), F32)
         rest = line
@@ -340,18 +356,52 @@
         if k:
             z_back[k] = remote(pick_out.at[k], pick_in.at[k], pair(zb_sem, k), mz ^ k, mn)
 
-    last = n_wide - 1
-    for k in range(n_wide + 4):
-        if k <= last:
-            make_slots(k)
-        if 1 <= k <= last + 1:
-            expert(k - 1)
-        if 3 <= k <= last + 3:
-            pick(k - 3)
-        if k <= last:
-            share(k)
-        if 2 <= k <= last + 2:
-            give_back(k - 2)
+    def share_dy(k):
+        share(k, 1, dy_rows, sd_sem)
+
+    def share_x(k):
+        share(k, 0, x_hbm, sx_sem)
+
+    slots_dy(0)
+    pack_x(0)
+    pack_x(1)
+    pack_dy(3)
+    share_dy(0)
+    slots_x(0)
+    slots_dy(1)
+    z_dy[2].wait_send()
+    start_dy(3)
+    start_x(1)
+    slots_dy(2)
+    pack_x(2)
+    pack_x(3)
+    expert(0)
+    share_dy(1)
+    share_x(0)
+    expert(1)
+    share_dy(2)
+    give_back(0)
+    slots_dy(3)
+    z_dy[3].wait_send()
+    start_x(2)
+    expert(2)
+    give_back(1)
+    slots_x(1)
+    share_dy(3)
+    pick(0)
+    expert(3)
+    give_back(2)
+    z_x[2].wait_send()
+    start_x(3)
+    pick(1)
+    slots_x(2)
+    give_back(3)
+    share_x(1)
+    pick(2)
+    share_x(2)
+    slots_x(3)
+    pick(3)
+    share_x(3)
 
     total = jnp.dot(spread_ref[0], pick_out[0], preferred_element_type=F32)
     for k in range(1, n_wide):
@@ -360,7 +410,7 @@
     out_ref[...] = total.astype(BF)
 
     for k in range(n_wide):
-        kept[k][1].wait()
+        kept_x[k].wait()
         for q in range(spots):
             shared[k, q, 0].wait_recv()
             shared[k, q, 0].wait_send()
@@ -371,7 +421,10 @@
                 returned[k, q].wait_send()
         halves[k].wait_send()
         if k:
-            z_copies[k].wait_send()
+            if k == 1:
+                z_dy[k].wait_send()
+            if k != 2:
+                z_x[k].wait_send()
             z_back[k].wait_send()
     for copy in saves:
         copy.wait()
@@ -383,10 +436,10 @@
     spots = n_narrow // 2
     count, width = tokens.shape
     rows = pack.shape[1]
-    half = w_gate.shape[2]
-    cap = gate_saved.shape[1] // devices
+    half = w_gate.shape[1]
+    cap = gate_saved.shape[2] // devices
     chunk = n_narrow * cap
-    wide_row = 2 * width + info.shape[2]
+    wide_row = width + info.shape[2]
     flops = 6 * devices * cap * width * half
     vmem = pl.BlockSpec(memory_space=pltpu.VMEM)
     hbm = pl.BlockSpec(memory_space=pl.ANY)
@@ -397,24 +450,28 @@
             jax.ShapeDtypeStruct((count, width), BF),
             jax.ShapeDtypeStruct((devices, cap, width), BF),
             jax.ShapeDtypeStruct((devices, cap, width), BF),
-            jax.ShapeDtypeStruct((devices * cap, half), BF),
-            jax.ShapeDtypeStruct((devices * cap, half), BF),
+            jax.ShapeDtypeStruct((half, devices * cap), BF),
+            jax.ShapeDtypeStruct((half, devices * cap), BF),
         ),
         in_specs=[vmem] * 5 + [hbm] * 5,
         out_specs=(vmem, hbm, hbm, hbm, hbm),
         scratch_shapes=[
+            pltpu.VMEM((n_wide, rows, width), BF),
             pltpu.VMEM((n_wide, rows, wide_row), BF),
+            pltpu.VMEM((n_wide, rows, width), BF),
             pltpu.VMEM((n_wide, rows, wide_row), BF),
             pltpu.VMEM((n_wide, spots, cap, width), BF),
             pltpu.VMEM((n_wide, spots, cap, width), BF),
             pltpu.VMEM((devices, cap, width), BF),
-            pltpu.VMEM((width, half), BF),
-            pltpu.VMEM((width, half), BF),
             pltpu.VMEM((half, width), BF),
-            pltpu.VMEM((n_wide, chunk, half), BF),
-            pltpu.VMEM((n_wide, chunk, half), BF),
-            pltpu.VMEM((n_wide, chunk, half), BF),
-            pltpu.VMEM((n_wide, chunk, half), BF),
+            pltpu.VMEM((half, width), BF),
+            pltpu.VMEM((half, width), BF),
+            pltpu.VMEM((n_wide, half, chunk), BF),
+            pltpu.VMEM((n_wide, half, chunk), BF),
+            pltpu.VMEM((n_wide, half, chunk), BF),
+            pltpu.VMEM((n_wide, half, chunk), BF),
+            pltpu.VMEM((chunk, half), BF),
+            pltpu.VMEM((chunk, half), BF),
             pltpu.VMEM((n_wide, 2, spots, cap, width), BF),
             pltpu.VMEM((n_wide, spots, cap, width), BF),
             pltpu.VMEM((n_wide, spots, cap, width), BF),
@@ -423,6 +480,7 @@
             sem((3 + 2 * n_wide,)),
             sem((n_wide, 3)),
             sem((n_wide, 3)),
+            sem((2, n_wide)),
             sem((2, n_wide)),
             sem((2, n_wide, spots)),
             sem((2, n_wide, spots)),
@@ -462,22 +520,25 @@
     info = jnp.take(info, groups, axis=1).astype(BF).transpose(1, 0, 2)
     info = jnp.pad(info, ((0, 0), (0, 0), (0, 128 - 2 * spots)))
     info = jnp.einsum("krt,ktc->krc", pack, info, preferred_element_type=F32).astype(BF)
+    turned_gate, turned_up = gate_saved.swapaxes(1, 2), up_saved.swapaxes(1, 2)
     token_grad, rows_x, rows_dy, gate_grad, up_grad = exchange(
-        tokens, out_grad, pack, spread, info, w_gate, w_up, w_down, gate_saved, up_saved
+        tokens, out_grad, pack, spread, info, w_gate.swapaxes(1, 2), w_up.swapaxes(1, 2), w_down,
+        turned_gate, turned_up,
     )
     rows_x = rows_x.reshape(devices * cap, width)
     rows_dy = rows_dy.reshape(devices * cap, width)
-    act = (jax.nn.silu(gate_saved[0].astype(F32)) * up_saved[0].astype(F32)).astype(BF)
-    grad_gate = lax.dot_general(rows_x, gate_grad, ACROSS, preferred_element_type=F32).astype(BF)
-    grad_up = lax.dot_general(rows_x, up_grad, ACROSS, preferred_element_type=F32).astype(BF)
-    grad_down = lax.dot_general(act, rows_dy, ACROSS, preferred_element_type=F32).astype(BF)
-    return (token_grad, grad_gate[None], grad_up[None], grad_down[None])
+    act = (jax.nn.silu(turned_gate[0].astype(F32)) * turned_up[0].astype(F32)).astype(BF)
+    grad_gate = jnp.dot(gate_grad, rows_x, preferred_element_type=F32).astype(BF)
+    grad_up = jnp.dot(up_grad, rows_x, preferred_element_type=F32).astype(BF)
+    grad_down = jnp.dot(act, rows_dy, preferred_element_type=F32).astype(BF)
+    return (token_grad, grad_gate.T[None], grad_up.T[None], grad_down[None])
 
 
 def local(tokens, out_grad, expert_ids, gates, w_gate, w_up, w_down, gate_saved, up_saved):
     slots = gate_saved.shape[1]
     cap = slots // (lax.axis_size("wide") * lax.axis_size("narrow"))
     fits = 8 * slots * tokens.shape[1] <= VMEM_BYTES and cap % 16 == 0
+    fits = fits and lax.axis_size("wide") == 4
     body = local_kernel if fits else local_permutes
     return body(tokens, out_grad, expert_ids, gates, w_gate, w_up, w_down, gate_saved, up_saved)
 

time: 195 us -> 157 us (0.81)
  the two profiles are of different devices: /device:TPU:0 before, /device:TPU:16 now
where the time goes in v3:
time: 157 us
  Pallas kernels  127 us (81%)
  matrix products  23.4 us (15%)
  other arithmetic  3.77 us (2%)
  local copies, waits for them, and re-layouts  1.96 us (1%)
    pallas_call x1, Pallas kernels, exchange(): pl.pallas_call(functools.partial(exchange_kernel, n_wide, n_narrow, cap),...  127 us
    dot_general x1, matrix products, local_kernel(): jnp.dot(gate_grad, rows_x, preferred_element_type=F32).astype(BF)  9.79 us
    dot_general x1, matrix products, local_kernel(): grad_down = jnp.dot(act, rows_dy, preferred_element_type=F32).astype(BF)  6.47 us
    dot_general x1, matrix products, local_kernel(): grad_up = jnp.dot(up_grad, rows_x, preferred_element_type=F32).astype(BF)  6.05 us

profile of v3, /device:TPU:16, one launch (start us, length us, event | category | flops | bytes accessed | tf_op | source)
XLA Modules:
  0.0 157.0 jit_solution(17346293998268433563)
XLA Ops:
  0.7 0.7 fusion.15
  1.4 0.1 convolution_select_fusion
  1.5 0.6 gather_fusion
  2.1 0.1 broadcast_select_fusion
  2.2 0.1 and_select_fusion
  2.3 0.7 convert_element_type.52
  3.0 0.7 select_reduce_fusion
  3.7 0.6 gather_fusion.1
  4.3 0.1 select_convert_fusion
  4.4 0.8 convolution_convert_fusion.3.info_ref
  5.2 0.7 fusion.11.pack_ref
  5.9 0.8 fusion.10.spread_ref
  6.7 127.2 %shard_map.120 = (bf16[128,2048]{1,0:T(8,128)(2,1)}, bf16[32,48,2048]{2,1,0:T(8,128)(2,1)}, bf16[32,48,2048]{2,1,0:T(8,128)(2,1)}, bf16[704,1536]{1,0:T(8,128)(2,1)}, bf16[704,1536]{1,0:T(8,128)(2,1)}) custom-call(bf16[128,2048]{1,0:T(8,128)(2,1)} %tokens_ref.1, bf16[128,2048]{1,0:T(8,128)(2,1)} %grad_ref.1, bf16[4,96,128]{2,1,0:T(8,128)(2,1)} %fusion.11.pack_ref, ...), custom_call_target="tpu_custom_call" | custom-call | flops 13287555072 | bytes 40000000 | tf_op jit(solution)/shard_map/pallas_call | solution.py:447
  133.8 0.0 copy-start.3
  133.8 0.0 copy-start.4
  133.8 0.0 slice-start
  133.8 9.8 %fusion.6 = bf16[1,2048,704]{1,2,0:T(8,128)(2,1)} fusion(bf16[704,1536]{1,0:T(8,128)(2,1)} %get-tuple-element.11, bf16[1536,2048]{1,0:T(8,128)(2,1)} %bitcast.45), kind=kOutput, calls=%fused_computation.13 | convolution fusion | flops 4430626816 | bytes 11337728 | tf_op jit(solution)/shard_map/dot_general | solution.py:531
  143.6 0.0 copy-done.3
  143.6 0.0 copy-done.4
  143.6 0.0 copy-start.1
  143.6 0.0 copy-start.2
  143.7 0.0 slice-start.1
  143.7 6.0 %fusion.7 = bf16[1,2048,704]{1,2,0:T(8,128)(2,1)} fusion(bf16[704,1536]{1,0:T(8,128)(2,1)S(1)} %copy-done.4, bf16[1536,2048]{1,0:T(8,128)(2,1)S(1)} %bitcast.46), kind=kOutput, calls=%fused_computation.14 | convolution fusion | flops 4430626816 | bytes 11337728 | tf_op jit(solution)/shard_map/dot_general | solution.py:532
  149.7 0.0 slice-done
  149.7 0.0 copy-done.1
  149.7 0.0 copy-done.2
  149.7 0.0 slice-done.1
  149.7 0.0 copy-start
  149.8 6.5 %fusion.5 = bf16[1,704,2048]{2,1,0:T(8,128)(2,1)} fusion(bf16[1536,2048]{1,0:T(8,128)(2,1)S(1)} %bitcast.44, bf16[1,1536,704]{1,2,0:T(8,128)(2,1)S(1)} %copy-done.2, bf16[1,1536,704]{1,2,0:T(8,128)(2,1)S(1)} %copy-done.1), kind=kOutput, calls=%fused_computation.12 | convolution fusion | flops 4439277568 | bytes 13500416 | tf_op jit(solution)/shard_map/dot_general | solution.py:533
  156.2 0.0 copy-done
  156.2 0.8 copy.26
  (6 shorter events, 0.1 us)
Async XLA Ops:
  133.8 9.8 %copy-start.3 = (bf16[32,48,2048]{2,1,0:T(8,128)(2,1)S(1)}, bf16[32,48,2048]{2,1,0:T(8,128)(2,1)}, u32[]{:S(2)}) copy-start(bf16[32,48,2048]{2,1,0:T(8,128)(2,1)} %get-tuple-element.10) | copy-start | bytes 18874372
  133.8 9.8 %copy-start.4 = (bf16[704,1536]{1,0:T(8,128)(2,1)S(1)}, bf16[704,1536]{1,0:T(8,128)(2,1)}, u32[]{:S(2)}) copy-start(bf16[704,1536]{1,0:T(8,128)(2,1)} %get-tuple-element.12) | copy-start | bytes 6488068
  133.8 15.9 %slice-start = ((s8[6291456]{0:T(1024)(128)(4,1)}), s8[4194304]{0:T(1024)(128)(4,1)S(1)}, s32[]{:S(2)}) async-start(s8[6291456]{0:T(1024)(128)(4,1)} %bitcast.42), calls=%async_computation | async-start | bytes 8388608
  143.6 6.1 %copy-start.1 = (bf16[1,1536,704]{1,2,0:T(8,128)(2,1)S(1)}, bf16[1,1536,704]{1,2,0:T(8,128)(2,1)}, u32[]{:S(2)}) copy-start(bf16[1,1536,704]{1,2,0:T(8,128)(2,1)} %param.16) | copy-start | bytes 6488068
  143.6 6.1 %copy-start.2 = (bf16[1,1536,704]{1,2,0:T(8,128)(2,1)S(1)}, bf16[1,1536,704]{1,2,0:T(8,128)(2,1)}, u32[]{:S(2)}) copy-start(bf16[1,1536,704]{1,2,0:T(8,128)(2,1)} %param.17) | copy-start | bytes 6488068
  143.7 6.1 %slice-start.1 = ((s8[6291456]{0:T(1024)(128)(4,1)}), s8[2097152]{0:T(1024)(128)(4,1)S(1)}, s32[]{:S(2)}) async-start(s8[6291456]{0:T(1024)(128)(4,1)} %bitcast.42), calls=%async_computation.1 | async-start | bytes 4194304
  149.7 6.5 %copy-start = (bf16[128,2048]{1,0:T(8,128)(2,1)S(1)}, bf16[128,2048]{1,0:T(8,128)(2,1)}, u32[]{:S(2)}) copy-start(bf16[128,2048]{1,0:T(8,128)(2,1)} %get-tuple-element.18) | copy-start | bytes 1572868

commit v4 on v3

--- a/solution.py
+++ b/solution.py
@@ -12,7 +12,7 @@
 ACROSS = (((0,), (0,)), ((), ()))
 INNER = (((1,), (1,)), ((), ()))
 MESH = pl.DeviceIdType.MESH
-VMEM_BYTES = 61 * 1024 * 1024
+VMEM_BYTES = 63 * 1024 * 1024
 
 
 def swap(value, axis, shift):
@@ -141,7 +141,8 @@
 
 def exchange_kernel(
     n_wide, n_narrow, cap, tokens_ref, grad_ref, pack_ref, spread_ref, info_ref, wg_hbm, wu_hbm,
-    wd_hbm, gate_hbm, up_hbm, out_ref, x_hbm, dy_hbm, gg_hbm, ug_hbm, send_x, send_dy, zx, zdy,
+    wd_hbm, gate_hbm, up_hbm, out_ref, x_last, down_hbm, gate_part,
+    up_part, gg_hbm, ug_hbm, x_rows, send_x, send_dy, zx, zdy,
     stage_x, stage_dy, dy_rows, w_gate, w_up, w_down, gate_in, up_in, gg, ug, gg_rows, ug_rows, part, half_in, back, pick_out, pick_in,
     load_sem, keep_sem, save_sem, zx_sem, zdy_sem, px_sem, pd_sem, sx_sem, sd_sem, half_sem, back_sem, zb_sem,
 ):
@@ -255,6 +256,9 @@
             stage_dy.at[k, ms], dy_rows.at[to], pair(sd_sem, k, 0), mz, sibling
         )
 
+    def x_at(k, n):
+        return x_last.at[n] if k == n_wide - 1 else x_rows.at[k, n]
+
     def slots_x(k):
         if k:
             z_x[k].wait_recv()
@@ -263,21 +267,22 @@
         stage_x[k] = jnp.dot(table, got[k], preferred_element_type=F32).astype(BF).reshape(
             spots, cap, width
         )
-        to = (mz ^ k) * n_narrow + mn
+        to = x_at(k, mn)
         for q in range(1, spots):
             plane[k, q, 0] = remote(
-                stage_x.at[k, ms ^ q], x_hbm.at[to], pair(px_sem, k, q), mz, plane_id(q)
+                stage_x.at[k, ms ^ q], to, pair(px_sem, k, q), mz, plane_id(q)
             )
-        kept_x[k] = here(stage_x.at[k, ms], x_hbm.at[to], keep_sem.at[k, 1])
-        shared[k, 0, 0] = remote(stage_x.at[k, ms], x_hbm.at[to], pair(sx_sem, k, 0), mz, sibling)
-
-    def share(k, which, rows_ref, sem):
+        kept_x[k] = here(stage_x.at[k, ms], to, keep_sem.at[k, 1])
+        shared[k, 0, 0] = remote(stage_x.at[k, ms], to, pair(sx_sem, k, 0), mz, sibling)
+
+    def share(k, which, sem):
         for q in range(1, spots):
             plane[k, q, which].wait_recv()
-            at = (mz ^ k) * n_narrow + plane_id(q)
-            shared[k, q, which] = remote(
-                rows_ref.at[at], rows_ref.at[at], pair(sem, k, q), mz, sibling
-            )
+            if which:
+                at = dy_rows.at[(mz ^ k) * n_narrow + plane_id(q)]
+            else:
+                at = x_at(k, plane_id(q))
+            shared[k, q, which] = remote(at, at, pair(sem, k, q), mz, sibling)
 
     halves = [None] * n_wide
     saves = []
@@ -302,10 +307,10 @@
         gg[k] = gate_grad.astype(BF)
         ug_rows[...] = jnp.transpose(ug[k])
         gg_rows[...] = jnp.transpose(gg[k])
-        source_rows = pl.ds(pl.multiple_of((mz ^ k) * chunk, 128), chunk)
-        saves.append(here(gg.at[k], gg_hbm.at[:, source_rows], save_sem.at[k, 0]))
-        saves.append(here(ug.at[k], ug_hbm.at[:, source_rows], save_sem.at[k, 1]))
-        saves.append(here(dy_rows.at[source], dy_hbm.at[source], save_sem.at[k, 2]))
+        gate_in[k] = (gate_pre * sigma * up_pre).astype(BF)
+        if k == n_wide - 1:
+            saves.append(here(gg.at[k], gg_hbm, save_sem.at[0]))
+            saves.append(here(ug.at[k], ug_hbm, save_sem.at[1]))
         if k == 0:
             loads[1].wait()
             loads[2].wait()
@@ -357,10 +362,47 @@
             z_back[k] = remote(pick_out.at[k], pick_in.at[k], pair(zb_sem, k), mz ^ k, mn)
 
     def share_dy(k):
-        share(k, 1, dy_rows, sd_sem)
+        share(k, 1, sd_sem)
 
     def share_x(k):
-        share(k, 0, x_hbm, sx_sem)
+        share(k, 0, sx_sem)
+
+    wide_tile = 512
+
+    def down_tile(j, carry):
+        at = pl.ds(pl.multiple_of(j * wide_tile, wide_tile), wide_tile)
+        value = jnp.zeros((w_down.shape[0], wide_tile), F32)
+        for k in range(n_wide):
+            rows_of = dy_rows[pl.ds((mz ^ k) * n_narrow, n_narrow), :, at]
+            value = value + jnp.dot(
+                gate_in[k], rows_of.reshape(chunk, wide_tile), preferred_element_type=F32
+            )
+        w_down[:, at] = value.astype(BF)
+        return carry
+
+    def multiply_down(first, last):
+        lax.fori_loop(first, last, down_tile, 0)
+        if last == width // wide_tile:
+            saves.append(here(w_down, down_hbm, save_sem.at[2]))
+
+    def multiply_x(left, target):
+        def tile_of(j, carry):
+            at = pl.ds(pl.multiple_of(j * wide_tile, wide_tile), wide_tile)
+            value = jnp.zeros((w_gate.shape[0], wide_tile), F32)
+            for k in range(n_wide - 1):
+                value = value + jnp.dot(
+                    left[k], x_rows[k, :, :, at].reshape(chunk, wide_tile),
+                    preferred_element_type=F32,
+                )
+            target[:, at] = value.astype(BF)
+            return carry
+
+        lax.fori_loop(0, width // wide_tile, tile_of, 0)
+
+    def have_x(k):
+        kept_x[k].wait()
+        for q in range(spots):
+            shared[k, q, 0].wait_recv()
 
     slots_dy(0)
     pack_x(0)
@@ -397,11 +439,20 @@
     slots_x(2)
     give_back(3)
     share_x(1)
+    multiply_down(0, 2)
     pick(2)
     share_x(2)
+    multiply_down(2, 4)
     slots_x(3)
+    for k in range(n_wide - 1):
+        have_x(k)
+    multiply_x(gg, w_gate)
+    saves.append(here(w_gate, gate_part, save_sem.at[3]))
     pick(3)
     share_x(3)
+    multiply_x(ug, w_up)
+    saves.append(here(w_up, up_part, save_sem.at[4]))
+    have_x(n_wide - 1)
 
     total = jnp.dot(spread_ref[0], pick_out[0], preferred_element_type=F32)
     for k in range(1, n_wide):
@@ -410,9 +461,7 @@
     out_ref[...] = total.astype(BF)
 
     for k in range(n_wide):
-        kept_x[k].wait()
         for q in range(spots):
-            shared[k, q, 0].wait_recv()
             shared[k, q, 0].wait_send()
             shared[k, q, 1].wait_send()
             if q:
@@ -448,14 +497,17 @@
         functools.partial(exchange_kernel, n_wide, n_narrow, cap),
         out_shape=(
             jax.ShapeDtypeStruct((count, width), BF),
-            jax.ShapeDtypeStruct((devices, cap, width), BF),
-            jax.ShapeDtypeStruct((devices, cap, width), BF),
-            jax.ShapeDtypeStruct((half, devices * cap), BF),
-            jax.ShapeDtypeStruct((half, devices * cap), BF),
+            jax.ShapeDtypeStruct((n_narrow, cap, width), BF),
+            jax.ShapeDtypeStruct((half, width), BF),
+            jax.ShapeDtypeStruct((half, width), BF),
+            jax.ShapeDtypeStruct((half, width), BF),
+            jax.ShapeDtypeStruct((half, chunk), BF),
+            jax.ShapeDtypeStruct((half, chunk), BF),
         ),
         in_specs=[vmem] * 5 + [hbm] * 5,
-        out_specs=(vmem, hbm, hbm, hbm, hbm),
+        out_specs=(vmem, hbm, hbm, hbm, hbm, hbm, hbm),
         scratch_shapes=[
+            pltpu.VMEM((n_wide - 1, n_narrow, cap, width), BF),
             pltpu.VMEM((n_wide, rows, width), BF),
             pltpu.VMEM((n_wide, rows, wide_row), BF),
             pltpu.VMEM((n_wide, rows, width), BF),
@@ -479,7 +531,7 @@
             pltpu.VMEM((n_wide, rows, width), BF),
             sem((3 + 2 * n_wide,)),
             sem((n_wide, 3)),
-            sem((n_wide, 3)),
+            sem((5,)),
             sem((2, n_wide)),
             sem((2, n_wide)),
             sem((2, n_wide, spots)),
@@ -521,17 +573,14 @@
     info = jnp.pad(info, ((0, 0), (0, 0), (0, 128 - 2 * spots)))
     info = jnp.einsum("krt,ktc->krc", pack, info, preferred_element_type=F32).astype(BF)
     turned_gate, turned_up = gate_saved.swapaxes(1, 2), up_saved.swapaxes(1, 2)
-    token_grad, rows_x, rows_dy, gate_grad, up_grad = exchange(
+    token_grad, rows_x, grad_down, gate_part, up_part, gate_grad, up_grad = exchange(
         tokens, out_grad, pack, spread, info, w_gate.swapaxes(1, 2), w_up.swapaxes(1, 2), w_down,
-        turned_gate, turned_up,
+        gate_saved.swapaxes(1, 2), up_saved.swapaxes(1, 2),
     )
-    rows_x = rows_x.reshape(devices * cap, width)
-    rows_dy = rows_dy.reshape(devices * cap, width)
-    act = (jax.nn.silu(turned_gate[0].astype(F32)) * turned_up[0].astype(F32)).astype(BF)
-    grad_gate = jnp.dot(gate_grad, rows_x, preferred_element_type=F32).astype(BF)
-    grad_up = jnp.dot(up_grad, rows_x, preferred_element_type=F32).astype(BF)
-    grad_down = jnp.dot(act, rows_dy, preferred_element_type=F32).astype(BF)
-    return (token_grad, grad_gate.T[None], grad_up.T[None], grad_down[None])
+    rows_x = rows_x.reshape(n_narrow * cap, width)
+    grad_gate = jnp.dot(gate_grad, rows_x, preferred_element_type=F32) + gate_part.astype(F32)
+    grad_up = jnp.dot(up_grad, rows_x, preferred_element_type=F32) + up_part.astype(F32)
+    return (token_grad, grad_gate.astype(BF).T[None], grad_up.astype(BF).T[None], grad_down[None])
 
 
 def local(tokens, out_grad, expert_ids, gates, w_gate, w_up, w_down, gate_saved, up_saved):

time: 157 us -> 146 us (0.930)
  the two profiles are of different devices: /device:TPU:16 before, /device:TPU:0 now
where the time goes in v4:
time: 146 us; the launch traced here: 143 us
  Pallas kernels  125 us (86%)
  matrix products  10.2 us (7%)
  other arithmetic  3.77 us (3%)
  local copies, waits for them, and re-layouts  3.53 us (2%)
    pallas_call x1, Pallas kernels, exchange(): pl.pallas_call(functools.partial(exchange_kernel, n_wide, n_narrow, cap),...  125 us
    dot_general x1, matrix products, local_kernel(): jnp.dot(gate_grad, rows_x, preferred_element_type=F32)  5.84 us
    dot_general x1, matrix products, local_kernel(): jnp.dot(up_grad, rows_x, preferred_element_type=F32) + up_part.astype(F32)  3.27 us

profile of v4, /device:TPU:0, one launch (start us, length us, event | category | flops | bytes accessed | tf_op | source)
XLA Modules:
  0.0 143.5 jit_solution(9606246053013599887)
XLA Ops:
  0.7 0.7 fusion.7
  1.4 0.1 convolution_select_fusion
  1.5 0.6 gather_fusion
  2.1 0.1 broadcast_select_fusion
  2.2 0.1 and_select_fusion
  2.3 0.7 convert_element_type.39
  3.0 0.7 select_reduce_fusion
  3.7 0.6 gather_fusion.1
  4.3 0.1 select_convert_fusion
  4.4 0.8 convolution_convert_fusion.info_ref
  5.2 0.7 fusion.3.pack_ref
  5.9 0.8 fusion.2.spread_ref
  6.7 125.3 %shard_map.120 = (bf16[128,2048]{1,0:T(8,128)(2,1)}, bf16[8,48,2048]{2,1,0:T(8,128)(2,1)}, bf16[704,2048]{1,0:T(8,128)(2,1)}, bf16[704,2048]{1,0:T(8,128)(2,1)},...) custom-call(bf16[128,2048]{1,0:T(8,128)(2,1)} %tokens_ref.1, ...), custom_call_target="tpu_custom_call" | custom-call | flops 13287555072 | bytes 40000000 | tf_op jit(solution)/shard_map/pallas_call | solution.py:496
  131.9 0.0 copy-start.2
  131.9 0.0 copy-start.3
  131.9 0.0 copy-start.4
  131.9 5.8 %fusion = bf16[1,2048,704]{1,2,0:T(8,128)(2,1)} fusion(bf16[704,2048]{1,0:T(8,128)(2,1)} %get-tuple-element.14, bf16[704,384]{1,0:T(8,128)(2,1)} %get-tuple-element.12, bf16[384,2048]{1,0:T(8,128)(2,1)} %bitcast.33), kind=kOutput, calls=%fused_computation.4 | convolution fusion | flops 1111621632 | bytes 7880704 | tf_op jit(solution)/shard_map/dot_general | solution.py:581
  137.8 0.0 copy-done.2
  137.8 0.0 copy-done.3
  137.8 0.0 copy-done.4
  137.8 0.0 copy-start.1
  137.8 0.0 copy-start
  137.8 3.3 %fusion.1 = bf16[1,2048,704]{1,2,0:T(8,128)(2,1)} fusion(bf16[704,2048]{1,0:T(8,128)(2,1)S(1)} %copy-done.3, bf16[704,384]{1,0:T(8,128)(2,1)S(1)} %copy-done.4, bf16[384,2048]{1,0:T(8,128)(2,1)S(1)} %bitcast.34), kind=kOutput, calls=%fused_computation.5 | convolution fusion | flops 1111621632 | bytes 7880704 | tf_op jit(solution)/shard_map/dot_general | solution.py:582
  141.1 0.0 copy-done.1
  141.1 0.8 copy.27
  141.9 0.0 copy-done
  141.9 1.6 %copy.28 = bf16[1,704,2048]{2,1,0:T(8,128)(2,1)} copy(bf16[1,704,2048]{2,1,0:T(8,128)(2,1)S(1)} %bitcast.25) | data formatting | bytes 5767168
  (5 shorter events, 0.1 us)
Async XLA Ops:
  131.9 5.9 %copy-start.2 = (bf16[8,48,2048]{2,1,0:T(8,128)(2,1)S(1)}, bf16[8,48,2048]{2,1,0:T(8,128)(2,1)}, u32[]{:S(2)}) copy-start(bf16[8,48,2048]{2,1,0:T(8,128)(2,1)} %get-tuple-element.13) | copy-start | bytes 4718596
  131.9 5.9 %copy-start.3 = (bf16[704,2048]{1,0:T(8,128)(2,1)S(1)}, bf16[704,2048]{1,0:T(8,128)(2,1)}, u32[]{:S(2)}) copy-start(bf16[704,2048]{1,0:T(8,128)(2,1)} %get-tuple-element.16) | copy-start | bytes 8650756
  131.9 5.9 %copy-start.4 = (bf16[704,384]{1,0:T(8,128)(2,1)S(1)}, bf16[704,384]{1,0:T(8,128)(2,1)}, u32[]{:S(2)}) copy-start(bf16[704,384]{1,0:T(8,128)(2,1)} %get-tuple-element.15) | copy-start | bytes 1622020
  137.8 3.3 %copy-start.1 = (bf16[128,2048]{1,0:T(8,128)(2,1)S(1)}, bf16[128,2048]{1,0:T(8,128)(2,1)}, u32[]{:S(2)}) copy-start(bf16[128,2048]{1,0:T(8,128)(2,1)} %get-tuple-element.22) | copy-start | bytes 1572868
  137.8 4.1 %copy-start = (bf16[704,2048]{1,0:T(8,128)(2,1)S(1)}, bf16[704,2048]{1,0:T(8,128)(2,1)}, u32[]{:S(2)}) copy-start(bf16[704,2048]{1,0:T(8,128)(2,1)} %get-tuple-element.17) | copy-start | bytes 8650756

commit v5 on v4

--- a/solution.py
+++ b/solution.py
@@ -428,13 +428,12 @@
     start_x(2)
     expert(2)
     give_back(1)
+    start_x(3)
     slots_x(1)
     share_dy(3)
     pick(0)
     expert(3)
     give_back(2)
-    z_x[2].wait_send()
-    start_x(3)
     pick(1)
     slots_x(2)
     give_back(3)
@@ -472,8 +471,7 @@
         if k:
             if k == 1:
                 z_dy[k].wait_send()
-            if k != 2:
-                z_x[k].wait_send()
+            z_x[k].wait_send()
             z_back[k].wait_send()
     for copy in saves:
         copy.wait()

time: 146 us -> 146 us (level)
  no operation moved by 1% of the time
where the time goes in v5:
time: 146 us; the launch traced here: 143 us
  Pallas kernels  125 us (86%)
  matrix products  10.2 us (7%)
  other arithmetic  3.77 us (3%)
  local copies, waits for them, and re-layouts  3.53 us (2%)
    pallas_call x1, Pallas kernels, exchange(): pl.pallas_call(functools.partial(exchange_kernel, n_wide, n_narrow, cap),...  125 us
    dot_general x1, matrix products, local_kernel(): jnp.dot(gate_grad, rows_x, preferred_element_type=F32)  5.84 us
    dot_general x1, matrix products, local_kernel(): jnp.dot(up_grad, rows_x, preferred_element_type=F32) + up_part.astype(F32)  3.27 us

profile of v5, /device:TPU:0, one launch (start us, length us, event | category | flops | bytes accessed | tf_op | source)
XLA Modules:
  0.0 143.5 jit_solution(7862154621650953266)
XLA Ops:
  0.7 0.7 fusion.7
  1.4 0.1 convolution_select_fusion
  1.5 0.6 gather_fusion
  2.1 0.1 broadcast_select_fusion
  2.2 0.1 and_select_fusion
  2.3 0.7 convert_element_type.39
  3.0 0.7 select_reduce_fusion
  3.7 0.6 gather_fusion.1
  4.3 0.1 select_convert_fusion
  4.4 0.8 convolution_convert_fusion.info_ref
  5.2 0.7 fusion.3.pack_ref
  5.9 0.8 fusion.2.spread_ref
  6.7 125.3 %shard_map.120 = (bf16[128,2048]{1,0:T(8,128)(2,1)}, bf16[8,48,2048]{2,1,0:T(8,128)(2,1)}, bf16[704,2048]{1,0:T(8,128)(2,1)}, bf16[704,2048]{1,0:T(8,128)(2,1)},...) custom-call(bf16[128,2048]{1,0:T(8,128)(2,1)} %tokens_ref.1, ...), custom_call_target="tpu_custom_call" | custom-call | flops 13287555072 | bytes 40000000 | tf_op jit(solution)/shard_map/pallas_call | solution.py:494
  131.9 0.0 copy-start.2
  131.9 0.0 copy-start.3
  131.9 0.0 copy-start.4
  131.9 5.8 %fusion = bf16[1,2048,704]{1,2,0:T(8,128)(2,1)} fusion(bf16[704,2048]{1,0:T(8,128)(2,1)} %get-tuple-element.14, bf16[704,384]{1,0:T(8,128)(2,1)} %get-tuple-element.12, bf16[384,2048]{1,0:T(8,128)(2,1)} %bitcast.33), kind=kOutput, calls=%fused_computation.4 | convolution fusion | flops 1111621632 | bytes 7880704 | tf_op jit(solution)/shard_map/dot_general | solution.py:579
  137.8 0.0 copy-done.2
  137.8 0.0 copy-done.3
  137.8 0.0 copy-done.4
  137.8 0.0 copy-start.1
  137.8 0.0 copy-start
  137.8 3.3 %fusion.1 = bf16[1,2048,704]{1,2,0:T(8,128)(2,1)} fusion(bf16[704,2048]{1,0:T(8,128)(2,1)S(1)} %copy-done.3, bf16[704,384]{1,0:T(8,128)(2,1)S(1)} %copy-done.4, bf16[384,2048]{1,0:T(8,128)(2,1)S(1)} %bitcast.34), kind=kOutput, calls=%fused_computation.5 | convolution fusion | flops 1111621632 | bytes 7880704 | tf_op jit(solution)/shard_map/dot_general | solution.py:580
  141.1 0.0 copy-done.1
  141.1 0.8 copy.27
  141.9 0.0 copy-done
  141.9 1.6 %copy.28 = bf16[1,704,2048]{2,1,0:T(8,128)(2,1)} copy(bf16[1,704,2048]{2,1,0:T(8,128)(2,1)S(1)} %bitcast.25) | data formatting | bytes 5767168
  (5 shorter events, 0.1 us)
Async XLA Ops:
  131.9 5.9 %copy-start.2 = (bf16[8,48,2048]{2,1,0:T(8,128)(2,1)S(1)}, bf16[8,48,2048]{2,1,0:T(8,128)(2,1)}, u32[]{:S(2)}) copy-start(bf16[8,48,2048]{2,1,0:T(8,128)(2,1)} %get-tuple-element.13) | copy-start | bytes 4718596
  131.9 5.9 %copy-start.3 = (bf16[704,2048]{1,0:T(8,128)(2,1)S(1)}, bf16[704,2048]{1,0:T(8,128)(2,1)}, u32[]{:S(2)}) copy-start(bf16[704,2048]{1,0:T(8,128)(2,1)} %get-tuple-element.16) | copy-start | bytes 8650756
  131.9 5.9 %copy-start.4 = (bf16[704,384]{1,0:T(8,128)(2,1)S(1)}, bf16[704,384]{1,0:T(8,128)(2,1)}, u32[]{:S(2)}) copy-start(bf16[704,384]{1,0:T(8,128)(2,1)} %get-tuple-element.15) | copy-start | bytes 1622020
  137.8 3.3 %copy-start.1 = (bf16[128,2048]{1,0:T(8,128)(2,1)S(1)}, bf16[128,2048]{1,0:T(8,128)(2,1)}, u32[]{:S(2)}) copy-start(bf16[128,2048]{1,0:T(8,128)(2,1)} %get-tuple-element.22) | copy-start | bytes 1572868
  137.8 4.1 %copy-start = (bf16[704,2048]{1,0:T(8,128)(2,1)S(1)}, bf16[704,2048]{1,0:T(8,128)(2,1)}, u32[]{:S(2)}) copy-start(bf16[704,2048]{1,0:T(8,128)(2,1)} %get-tuple-element.17) | copy-start | bytes 8650756
